TPU v7x, 32 devices: a whole 2x2x4 slice. The times are simulated.
32 devices in a mesh: mid: 8 (over z, x), off: 4 (over y, core).
Axes of the slice: x: 2, y: 2, z: 4, core: 2. Of those that a mesh axis runs over, the one named last changes fastest.
Arguments:
- query_rows: bfloat16 [8192, 1024], P(('mid', 'off')), may hold values from -8 to 8
- key_rows: bfloat16 [8192, 1024], P(('mid', 'off')), may hold values from -8 to 8
- value_rows: bfloat16 [8192, 1024], P(('mid', 'off')), may hold values from -6 to 6
- grad_out: bfloat16 [8192, 1024], P(('mid', 'off')), may hold values from -15 to 15
- out_weight: bfloat16 [1024, 1024], replicated, may hold values from -0.1875 to 0.1875
- masked_rows: int32 [8192], P(('mid', 'off')), may hold values 0 or 1
- far_blocks: int32 [32, 2], replicated, may hold values from -1 to 31, as said below
Outputs:
- query_grad: bfloat16 [8192, 1024], P(('mid', 'off'))
- key_grad: bfloat16 [8192, 1024], P(('mid', 'off'))
- value_grad: bfloat16 [8192, 1024], P(('mid', 'off'))
- weight_grad: bfloat16 [1024, 1024], replicated
Inputs may be any that keep to these rules, and one draw needn't show every extreme that they name: `far_blocks`: row c lists the far key blocks of query block c, the same for every gather; entry 0 of a row is never -1, a row's listed blocks are distinct, and none is c - 1, c or c + 1. Taking the rows in aligned blocks of 8 (the query blocks of one device), the live entries of one such block name at most 4 key blocks of any one aligned group of 8 key blocks, and in every draw some pair of groups meets that bound exactly.
All inputs are finite; a program needn't handle non-finite values. No bound on the sum of `masked_rows` on one device may be relied on, other than what follows from the above.
Results may differ from a plain program's by a relative error of at most 0.018.
Values may be sent and summed in bfloat16 or wider, within the bound.
A program may use at most 128 MiB of HBM per device.

v0:
```python
import jax
import jax.numpy as jnp
from jax import lax
from jax.sharding import PartitionSpec as P

HEADS = 16
HEAD_DIM = 64
BLOCK = 32


def padded(cells, sides, width):
    for axis, dim in sides:
        count = lax.axis_size(axis)
        ends = count - 1
        head = lax.slice_in_dim(cells, 0, width, axis=dim)
        tail = lax.slice_in_dim(cells, cells.shape[dim] - width, cells.shape[dim], axis=dim)
        cells = jnp.concatenate(
            [
                lax.ppermute(tail, axis, [(i, (i + 1) % count) for i in range(ends)]),
                cells,
                lax.ppermute(head, axis, [((i + 1) % count, i) for i in range(ends)]),
            ],
            axis=dim,
        )
    return cells


def attend(query_blocks, key_sets, allowed, hit_grad, out_weight, scaling):
    blocks, block_rows, head_count, head_dim = query_blocks.shape
    key_count = key_sets.shape[1]
    features = head_count * head_dim
    key_part = key_sets[:, :, :features].reshape(blocks, key_count, head_count, head_dim)
    value_part = key_sets[:, :, features:].reshape(blocks, key_count, head_count, head_dim)
    scores = (
        jnp.einsum("nqhe,nkhe->nhqk", query_blocks, key_part, preferred_element_type=jnp.float32)
        * scaling
    )
    scores = jnp.where(allowed[:, None, None, :], scores, -jnp.inf)
    row_max = jnp.max(scores, axis=-1, keepdims=True)
    log_total = row_max + jnp.log(jnp.sum(jnp.exp(scores - row_max), axis=-1, keepdims=True))
    prob_full = jnp.exp(scores - log_total)
    prob_half = prob_full.astype(jnp.bfloat16)
    attended = jnp.einsum(
        "nhqk,nkhe->nqhe", prob_half, value_part, preferred_element_type=jnp.float32
    ).astype(jnp.bfloat16)
    flat_attended = attended.reshape(blocks * block_rows, features)
    weight_part = jnp.einsum(
        "ta,tb->ab", flat_attended, hit_grad, preferred_element_type=jnp.float32
    )
    attn_grad = jnp.einsum(
        "tb,ab->ta", hit_grad, out_weight, preferred_element_type=jnp.float32
    ).astype(jnp.bfloat16)
    grad_blocks = attn_grad.reshape(blocks, block_rows, head_count, head_dim)
    row_dot = jnp.sum(grad_blocks.astype(jnp.float32) * attended.astype(jnp.float32), axis=-1)
    row_dot = jnp.transpose(row_dot, (0, 2, 1))
    prob_grad = jnp.einsum(
        "nqhe,nkhe->nhqk", grad_blocks, value_part, preferred_element_type=jnp.float32
    )
    score_grad = (prob_full * (prob_grad - row_dot[..., None])).astype(jnp.bfloat16)
    query_grad = (
        jnp.einsum("nhqk,nkhe->nqhe", score_grad, key_part, preferred_element_type=jnp.float32)
        * scaling
    ).astype(jnp.bfloat16)
    return (query_grad, score_grad, prob_half, grad_blocks, weight_part, log_total[..., 0], row_dot)


def key_grads(score_grad, prob_half, query_blocks, grad_blocks, scaling):
    blocks = score_grad.shape[0]
    key_count = score_grad.shape[3]
    key_grad = (
        jnp.einsum("nhqk,nqhe->nkhe", score_grad, query_blocks, preferred_element_type=jnp.float32)
        * scaling
    )
    value_grad = jnp.einsum(
        "nhqk,nqhe->nkhe", prob_half, grad_blocks, preferred_element_type=jnp.float32
    )
    return jnp.concatenate(
        [key_grad.reshape(blocks, key_count, -1), value_grad.reshape(blocks, key_count, -1)],
        axis=-1,
    )


def band_totals(band_grads, blocks, block_rows):
    parts = band_grads.reshape(blocks, 3, block_rows, band_grads.shape[-1])
    totals = jnp.zeros((blocks + 2, block_rows, band_grads.shape[-1]), jnp.float32)
    totals = totals.at[:blocks].add(parts[:, 0])
    totals = totals.at[1 : blocks + 1].add(parts[:, 1])
    totals = totals.at[2:].add(parts[:, 2])
    return totals


def on_device(query_rows, key_rows, value_rows, grad_out, out_weight, masked_rows, far_blocks):
    off_size = lax.axis_size("off")
    mid_size = lax.axis_size("mid")
    position = lax.axis_index("off")
    row_count, features = query_rows.shape
    block_rows = BLOCK
    blocks = row_count // block_rows
    far_slots = far_blocks.shape[1]
    capacity = max(2, -(-(blocks * far_slots) // off_size))
    slot_total = off_size * capacity
    total_blocks = blocks * off_size
    scaling = HEAD_DIM ** (-0.5)
    hit_grad = grad_out * masked_rows[:, None].astype(jnp.bfloat16)
    query_blocks = query_rows.reshape(blocks, block_rows, HEADS, HEAD_DIM)
    pair_rows = jnp.concatenate([key_rows, value_rows], axis=1)
    pair_blocks = pair_rows.reshape(blocks, block_rows, 2 * features)
    extended = padded(pair_rows, (("off", 0),), block_rows)
    extended = extended.reshape(blocks + 2, block_rows, 2 * features)
    band_sets = jnp.concatenate([extended[:blocks], extended[1 : blocks + 1], extended[2:]], axis=1)
    global_block = position * blocks + jnp.arange(blocks)
    edge_ok = jnp.stack(
        [global_block >= 1, global_block >= 0, global_block <= total_blocks - 2], axis=1
    )
    far_table = far_blocks.reshape(off_size, blocks * far_slots)
    live_all = far_table >= 0
    owner_all = jnp.where(live_all, far_table // blocks, -1)
    owner_hits = (owner_all[:, :, None] == jnp.arange(off_size)[None, None, :]).astype(jnp.int32)
    rank_all = jnp.sum((jnp.cumsum(owner_hits, axis=1) - owner_hits) * owner_hits, axis=2)
    mine_live = lax.dynamic_index_in_dim(live_all, position, 0, keepdims=False)
    mine_owner = lax.dynamic_index_in_dim(owner_all, position, 0, keepdims=False)
    mine_rank = lax.dynamic_index_in_dim(rank_all, position, 0, keepdims=False)
    mine_slot = jnp.where(mine_live, mine_owner * capacity + mine_rank, slot_total)
    wanted = live_all & (owner_all == position)
    matches = wanted[:, :, None] & (rank_all[:, :, None] == jnp.arange(capacity)[None, None, :])
    local_ids = far_table - position * blocks
    chosen = jnp.sum(jnp.where(matches, local_ids[:, :, None], 0), axis=1).reshape(-1)
    filled = jnp.any(matches, axis=1).reshape(-1)
    outgoing = jnp.take(pair_blocks, chosen, axis=0)
    outgoing = jnp.where(filled[:, None, None], outgoing, jnp.zeros((), jnp.bfloat16))
    arrived = lax.all_to_all(
        outgoing.reshape(off_size, capacity, block_rows, 2 * features),
        "off",
        split_axis=0,
        concat_axis=0,
        tiled=True,
    )
    arrived = arrived.reshape(slot_total, block_rows, 2 * features)
    far_sets = jnp.take(arrived, jnp.where(mine_live, mine_slot, 0), axis=0)
    far_sets = far_sets.reshape(blocks, far_slots * block_rows, 2 * features)
    allowed = jnp.concatenate(
        [
            jnp.repeat(edge_ok, block_rows, axis=1),
            jnp.repeat(mine_live.reshape(blocks, far_slots), block_rows, axis=1),
        ],
        axis=1,
    )
    key_sets = jnp.concatenate([band_sets, far_sets], axis=1)
    query_grad, score_grad, prob_half, grad_blocks, weight_part, log_total, row_dot = attend(
        query_blocks, key_sets, allowed, hit_grad, out_weight, scaling
    )
    pair_grads = key_grads(score_grad, prob_half, query_blocks, grad_blocks, scaling)
    far_part = (
        pair_grads[:, 3 * block_rows :]
        .reshape(blocks * far_slots, block_rows, 2 * features)
        .astype(jnp.bfloat16)
    )
    outbound = (
        jnp.zeros((slot_total + 1, block_rows, 2 * features), jnp.bfloat16)
        .at[mine_slot]
        .set(far_part)[:slot_total]
    )
    inbound = lax.all_to_all(
        outbound.reshape(off_size, capacity, block_rows, 2 * features),
        "off",
        split_axis=0,
        concat_axis=0,
        tiled=True,
    )
    inbound = inbound.reshape(slot_total, block_rows * 2 * features)
    totals = band_totals(pair_grads[:, : 3 * block_rows], blocks, block_rows)
    own_grads = totals[1 : blocks + 1]
    edges = jnp.concatenate([totals[0], totals[blocks + 1]], axis=0)
    incoming = padded(edges.astype(jnp.bfloat16), (("off", 0),), block_rows).astype(edges.dtype)
    own_grads = own_grads.at[0].add(incoming[:block_rows])
    own_grads = own_grads.at[blocks - 1].add(incoming[3 * block_rows :])
    selector = ((chosen[None, :] == jnp.arange(blocks)[:, None]) & filled[None, :]).astype(
        jnp.bfloat16
    )
    far_total = jnp.einsum("ns,sx->nx", selector, inbound, preferred_element_type=jnp.float32)
    own_grads = own_grads + far_total.reshape(blocks, block_rows, 2 * features)
    own_grads = own_grads.reshape(row_count, 2 * features).astype(jnp.bfloat16)
    weight_scale = (row_count * mid_size * off_size) ** (-0.5)
    summed = lax.psum(weight_part, ("mid", "off"))
    weight_grad = (summed * weight_scale).astype(jnp.bfloat16)
    return (
        query_grad.reshape(row_count, features),
        own_grads[:, :features],
        own_grads[:, features:],
        weight_grad,
    )


def solution(mesh):
    return jax.shard_map(
        on_device,
        mesh=mesh,
        in_specs=(
            P(("mid", "off"), None),
            P(("mid", "off"), None),
            P(("mid", "off"), None),
            P(("mid", "off"), None),
            P(),
            P(("mid", "off")),
            P(),
        ),
        out_specs=(P(("mid", "off"), None), P(("mid", "off"), None), P(("mid", "off"), None), P()),
        check_vma=False,
    )
```

profile of v0, /device:TPU:0, one launch (start us, length us, event | category | flops | bytes accessed | tf_op | source)
XLA Modules:
  0.0 306.4 jit_solution(7459329339275772287)
XLA Ops:
  11.1 2.0 gather_fusion
  13.1 3.2 %select_select_fusion = bf16[4,4,32,2048]{3,2,1,0:T(8,128)(2,1)} fusion(bf16[4,4,32,2048]{3,2,1,0:T(8,128)(2,1)} %bitcast.137, pred[4,4]{1,0:T(4,128)(4,1)S(1)} %compare_and_fusion.1, pred[4,4]{1,0:T(4,128)(4,1)S(1)} %fusion.32), kind=kLoop, calls=%fused_computation.33 | loop fusion | flops 2097152 | bytes 4194336 | tf_op jit(solution)/shard_map/jit(_where)/select_n | solution.py:130
  16.3 4.4 %all-to-all-start = ((bf16[4,4,32,2048]{3,2,1,0:T(8,128)(2,1)}), bf16[4,4,32,2048]{3,2,1,0:T(8,128)(2,1)}, u32[]{:S(2)}, u32[]{:S(2)}) async-start(bf16[4,4,32,2048]{3,2,1,0:T(8,128)(2,1)} %select_select_fusion), calls=%async_computation | async-start | bytes 4194304 | tf_op jit(solution)/shard_map/all_to_all | solution.py:131
  20.8 2.4 collective-permute-start
  23.1 1.3 collective-permute-start.1
  25.5 1.3 squeeze.20
  27.4 1.3 reduce.17
  33.5 2.6 convolution_convert_fusion.1
  36.8 1.2 and.82
  38.1 1.8 reshape.446
  39.9 2.0 reshape.447
  42.6 2.5 pad_maximum_fusion.3
  45.0 2.1 all-to-all-done
  47.1 3.6 %gather_fusion.1 = bf16[16,32,2048]{2,1,0:T(8,128)(2,1)} fusion(bf16[16,32,2048]{2,1,0:T(8,128)(2,1)} %bitcast.5, s32[1024]{0:T(1024)S(1)} %pad_clamp_fusion), kind=kCustom, calls=%fused_computation.1 | custom fusion | bytes 4194368 | tf_op jit(solution)/shard_map/jit(_take)/gather | solution.py:139
  50.7 2.0 bitcast_select_fusion
  52.9 5.0 %pad_maximum_fusion = bf16[8,160,2048]{2,1,0:T(8,128)(2,1)S(1)} fusion(bf16[8,64,2048]{2,1,0:T(8,128)(2,1)S(1)} %bitcast_select_fusion, bf16[8,32,2048]{2,1,0:T(8,128)(2,1)S(1)} %bitcast.141, bf16[8,32,2048]{2,1,0:T(8,128)(2,1)S(1)} %bitcast.133, bf16[8,32,2048]{2,1,0:T(8,128)(2,1)S(1)} %bitcast.140), kind=kLoop, calls=%fused_computation.6 | loop fusion | flops 20971520 | bytes 10485760 | tf_op jit(solution)/shard_map/concatenate | solution.py:148
  57.9 2.9 fusion.58
  60.8 6.0 %copy.23 = bf16[8,160,1024]{1,2,0:T(8,128)(2,1)} copy(bf16[8,160,1024]{2,1,0:T(8,128)(2,1)} %get-tuple-element.70) | data formatting | bytes 5242880 | tf_op jit(solution)/shard_map/slice | solution.py:32
  66.8 6.0 %copy.25 = bf16[8,160,1024]{1,2,0:T(8,128)(2,1)} copy(bf16[8,160,1024]{2,1,0:T(8,128)(2,1)} %get-tuple-element.69) | data formatting | bytes 5242880 | tf_op jit(solution)/shard_map/slice | solution.py:33
  72.8 3.2 %bitcast_reduce_fusion = (f32[8,16,32]{2,1,0:T(8,128)S(1)}, f32[8,16,160,32]{2,3,1,0:T(8,128)S(1)}) fusion(pred[8,160]{1,0:T(8,128)(4,1)S(1)} %pad_add_fusion, bf16[8,160,16,64]{1,3,2,0:T(8,128)(2,1)} %bitcast.125, bf16[8,32,16,64]{3,2,1,0:T(8,128)(2,1)S(1)} %reshape.446), kind=kOutput, calls=%fused_computation.11 | convolution fusion | flops 85848064 | bytes 5784832 | tf_op jit(solution)/shard_map/nqhe,nkhe->nhqk/dot_general | solution.py:35
  76.0 1.5 fusion.3
  77.6 4.2 %fusion.17 = f32[8,16,64,160]{3,2,1,0:T(8,128)} fusion(bf16[8,32,16,64]{3,2,1,0:T(8,128)(2,1)S(1)} %reshape.447, f32[8,16,160,32]{2,3,1,0:T(8,128)S(1)} %get-tuple-element.78, f32[8,16,32]{2,1,0:T(8,128)S(1)} %log_add_fusion, pred[8,160]{1,0:T(8,128)(4,1)S(1)} %pad_add_fusion), kind=kOutput, calls=%fused_computation.43 | convolution fusion | flops 86507520 | bytes 8406272 | tf_op jit(solution)/shard_map/nhqk,nqhe->nkhe/dot_general | solution.py:74
  81.8 2.7 multiply_reduce_fusion
  84.5 2.6 multiply_convert_fusion.1
  87.2 4.5 %broadcast_multiply_fusion = f32[8,16,160,64]{2,3,1,0:T(8,128)} fusion(bf16[8,16,32,160]{3,2,1,0:T(8,128)(2,1)S(1)} %multiply_convert_fusion.1, bf16[8,32,16,64]{3,2,1,0:T(8,128)(2,1)S(1)} %copy-done.7), kind=kOutput, calls=%fused_computation.16 | convolution fusion | flops 85196800 | bytes 7077888 | tf_op jit(solution)/shard_map/nhqk,nqhe->nkhe/dot_general | solution.py:71
  91.7 8.1 %copy.31 = f32[8,160,1024]{2,1,0:T(8,128)} copy(f32[8,160,1024]{1,2,0:T(8,128)} %bitcast.128) | data formatting | bytes 10485760 | tf_op jit(solution)/shard_map/reshape | solution.py:78
  99.8 8.1 %copy.32 = f32[8,160,1024]{2,1,0:T(8,128)} copy(f32[8,160,1024]{1,2,0:T(8,128)} %bitcast.127) | data formatting | bytes 10485760 | tf_op jit(solution)/shard_map/reshape | solution.py:78
  107.9 3.6 %fusion = f32[8,96,2048]{2,1,0:T(8,128)S(1)} fusion(f32[8,160,1024]{2,1,0:T(8,128)} %copy.31, f32[8,160,1024]{2,1,0:T(8,128)} %copy.32), kind=kLoop, calls=%fused_computation.5 | loop fusion | flops 1572864 | bytes 16777216 | tf_op jit(solution)/shard_map/concatenate | solution.py:77
  113.0 1.8 slice-done
  114.7 1.6 slice-done.2
  117.0 1.6 fusion.1
  118.6 1.3 collective-permute-start.3
  119.9 6.9 %collective-permute-start.2 = (bf16[32,2048]{1,0:T(8,128)(2,1)S(1)}, bf16[32,2048]{1,0:T(8,128)(2,1)}, u32[]{:S(2)}, u32[]{:S(2)}) collective-permute-start(bf16[32,2048]{1,0:T(8,128)(2,1)S(1)} %fusion.27), channel_id=1, source_target_pairs={{0,1},{1,2},{2,3},{4,5},{5,6},{6,7},{8,9},{9,10},{10,11},{12,13},{... | collective-permute-start | bytes 393224 | tf_op jit(solution)/shard_map/ppermute | solution.py:19
  126.8 1.6 broadcast_in_dim.114
  128.5 5.7 %scatter_fusion = bf16[17,32,2048]{2,1,0:T(8,128)(2,1)} fusion(bf16[17,32,2048]{2,1,0:T(8,128)(2,1)} %broadcast_in_dim.114, s32[16]{0:T(128)S(1)} %copy-done.13, bf16[16,32,2048]{2,1,0:T(8,128)(2,1)} %bitcast.139), kind=kCustom, calls=%fused_computation.2 | custom fusion | bytes 6291520 | tf_op jit(solution)/shard_map/scatter | solution.py:161
  134.2 3.2 %slice.234 = bf16[16,32,2048]{2,1,0:T(8,128)(2,1)} slice(bf16[17,32,2048]{2,1,0:T(8,128)(2,1)} %scatter_fusion), slice={[0:16], [0:32], [0:2048]} | slice | bytes 4194304 | tf_op jit(solution)/shard_map/slice | solution.py:159
  137.3 4.5 %all-to-all-start.1 = ((bf16[4,4,32,2048]{3,2,1,0:T(8,128)(2,1)}), bf16[4,4,32,2048]{3,2,1,0:T(8,128)(2,1)}, u32[]{:S(2)}, u32[]{:S(2)}) async-start(bf16[4,4,32,2048]{3,2,1,0:T(8,128)(2,1)} %bitcast.138), calls=%async_computation.1 | async-start | bytes 4194304 | tf_op jit(solution)/shard_map/all_to_all | solution.py:163
  141.9 1.6 copy.40
  143.5 1.5 reshape.460
  145.0 4.0 %fusion.20 = f32[1024,1024]{1,0:T(8,128)} fusion(bf16[256,1024]{1,0:T(8,128)(2,1)} %reshape.460, bf16[256,1024]{1,0:T(8,128)(2,1)} %param.20, bf16[256]{0:T(256)(128)(2,1)S(1)} %copy-done.17), kind=kOutput, calls=%fused_computation.46 | convolution fusion | flops 537133056 | bytes 5243392 | tf_op jit(solution)/shard_map/ta,tb->ab/dot_general | solution.py:47
  149.0 3.5 %fusion.13 = bf16[8,32,16,64]{3,1,2,0:T(8,128)(2,1)S(1)} fusion(bf16[8,160,16,64]{1,3,2,0:T(8,128)(2,1)} %bitcast.126, bf16[8,16,32,160]{3,2,1,0:T(8,128)(2,1)S(1)} %multiply_convert_fusion.1), kind=kOutput, calls=%fused_computation.36 | convolution fusion | flops 84410368 | bytes 4456448 | tf_op jit(solution)/shard_map/nhqk,nkhe->nqhe/dot_general | solution.py:61
  153.2 1.5 reshape.449
  155.7 2.5 copy.37
  158.6 6.2 %scatter-add.24 = f32[8,32,2048]{2,0,1:T(8,128)} dynamic-update-slice(f32[8,32,2048]{2,0,1:T(8,128)} %copy.37, f32[1,32,2048]{2,0,1:T(1,128)S(1)} %copy_add_fusion, s32[]{:T(128)} %constant.205.clone.1, s32[]{:T(128)} %constant.201.clone.1, s32[]{:T(128)} %constant.201.clone.1) | dynamic-update-slice | bytes 524292 | tf_op jit(solution)/shard_map/scatter-add | solution.py:176
  164.9 10.2 %all-to-all-done.1 = bf16[4,4,32,2048]{3,2,1,0:T(8,128)(2,1)} async-done(((bf16[4,4,32,2048]{3,2,1,0:T(8,128)(2,1)}), bf16[4,4,32,2048]{3,2,1,0:T(8,128)(2,1)}, u32[]{:S(2)}, u32[]{:S(2)}) %all-to-all-start.1) | async-done | bytes 2097184 | tf_op jit(solution)/shard_map/all_to_all | solution.py:163
  175.1 4.6 %fusion.6 = bf16[8,32,2048]{2,0,1:T(8,128)(2,1)S(1)} fusion(f32[8,32,2048]{2,0,1:T(8,128)} %scatter-add.24, s32[16]{0:T(128)S(1)} %copy-done.12, pred[16]{0:T(512)(128)(4,1)S(1)} %copy-done.15, bf16[2,8,32,2048]{3,2,1,0:T(8,128)(2,1)} %bitcast.45), kind=kOutput, calls=%fused_computation.21 | convolution fusion | flops 17826048 | bytes 5242960 | tf_op jit(solution)/shard_map/ns,sx->nx/dot_general | solution.py:180
  181.3 114.1 %all-reduce.3.cloned.1.call-done = f32[1024,1024]{1,0:T(8,128)} async-done(((f32[1024,1024]{1,0:T(8,128)}), f32[1024,1024]{1,0:T(8,128)}) %all-reduce.3.cloned.1.call-update) | async-done | bytes 4194320 | tf_op jit(solution)/shard_map/psum | solution.py:184
  295.4 4.1 %multiply_convert_fusion = bf16[1024,1024]{1,0:T(8,128)(2,1)} fusion(f32[1024,1024]{1,0:T(8,128)} %all-reduce.3.cloned.1.call-done), kind=kLoop, calls=%fused_computation.15 | loop fusion | flops 2097152 | bytes 6291456 | tf_op jit(solution)/shard_map/convert_element_type | solution.py:185
  (101 shorter events, 17.6 us)
Async XLA Ops:
  7.2 26.3 %copy-start = (bf16[1024,1024]{1,0:T(8,128)(2,1)S(1)}, bf16[1024,1024]{1,0:T(8,128)(2,1)}, u32[]{:S(2)}) copy-start(bf16[1024,1024]{1,0:T(8,128)(2,1)} %param.21) | copy-start | bytes 6291460
  8.8 4.2 %copy-start.14 = (pred[4,4]{1,0:T(4,128)(4,1)}, pred[4,4]{1,0:T(4,128)(4,1)S(1)}, u32[]{:S(2)}) copy-start(pred[4,4]{1,0:T(4,128)(4,1)S(1)} %fusion.32) | copy-start | bytes 52
  16.3 30.9 %all-to-all-start = ((bf16[4,4,32,2048]{3,2,1,0:T(8,128)(2,1)}), bf16[4,4,32,2048]{3,2,1,0:T(8,128)(2,1)}, u32[]{:S(2)}, u32[]{:S(2)}) async-start(bf16[4,4,32,2048]{3,2,1,0:T(8,128)(2,1)} %select_select_fusion), calls=%async_computation | async-start | bytes 4194304 | tf_op jit(solution)/shard_map/all_to_all | solution.py:131
  20.8 21.8 %collective-permute-start = (bf16[32,2048]{1,0:T(8,128)(2,1)S(1)}, bf16[32,2048]{1,0:T(8,128)(2,1)S(1)}, u32[]{:S(2)}, u32[]{:S(2)}) collective-permute-start(bf16[32,2048]{1,0:T(8,128)(2,1)S(1)} %get-tuple-element.75), channel_id=1, source_target_pairs={{0,1},{1,2},{2,3},{4,5},{5,6},{6,7},{8,9},{9,10},{10,11},{12,13},{... | collective-permute-start | bytes 393224 | tf_op jit(solution)/shard_map/ppermute | solution.py:19
  23.1 19.4 %collective-permute-start.1 = (bf16[32,2048]{1,0:T(8,128)(2,1)S(1)}, bf16[32,2048]{1,0:T(8,128)(2,1)}, u32[]{:S(2)}, u32[]{:S(2)}) collective-permute-start(bf16[32,2048]{1,0:T(8,128)(2,1)S(1)} %get-tuple-element.76), channel_id=1, source_target_pairs={{1,0},{2,1},{3,2},{5,4},{6,5},{7,6},{9,8},{10,9},{11,10},{13,12},{... | collective-permute-start | bytes 393224 | tf_op jit(solution)/shard_map/ppermute | solution.py:21
  30.9 5.1 %copy-start.10 = (pred[8,64]{1,0:T(8,128)(4,1)S(1)}, pred[8,64]{1,0:T(8,128)(4,1)}, u32[]{:S(2)}) copy-start(pred[8,64]{1,0:T(8,128)(4,1)} %reshape.445) | copy-start | bytes 1540
  30.9 5.1 %copy-start.11 = (pred[8,96]{1,0:T(8,128)(4,1)S(1)}, pred[8,96]{1,0:T(8,128)(4,1)}, u32[]{:S(2)}) copy-start(pred[8,96]{1,0:T(8,128)(4,1)} %reshape.444) | copy-start | bytes 2308
  31.7 1.8 copy-start.16
  39.9 32.9 %copy-start.6 = (bf16[8,32,16,64]{3,2,1,0:T(8,128)(2,1)}, bf16[8,32,16,64]{3,2,1,0:T(8,128)(2,1)S(1)}, u32[]{:S(2)}) copy-start(bf16[8,32,16,64]{3,2,1,0:T(8,128)(2,1)S(1)} %reshape.446) | copy-start | bytes 1572868
  41.9 39.8 %copy-start.5 = (bf16[8,32,16,64]{3,2,1,0:T(8,128)(2,1)}, bf16[8,32,16,64]{3,2,1,0:T(8,128)(2,1)S(1)}, u32[]{:S(2)}) copy-start(bf16[8,32,16,64]{3,2,1,0:T(8,128)(2,1)S(1)} %reshape.447) | copy-start | bytes 1572868
  50.7 2.0 copy-start.8
  50.7 2.2 copy-start.9
  77.5 4.2 %copy-start.4 = (bf16[8,160,1024]{1,2,0:T(8,128)(2,1)S(1)}, bf16[8,160,1024]{1,2,0:T(8,128)(2,1)}, u32[]{:S(2)}) copy-start(bf16[8,160,1024]{1,2,0:T(8,128)(2,1)} %copy.25) | copy-start | bytes 7864324
  84.5 2.7 copy-start.7
  111.9 2.8 slice-start
  111.9 4.4 %slice-start.2 = ((s8[5242880]{0:T(1024)(128)(4,1)}), s8[4194304]{0:T(1024)(128)(4,1)S(1)}, s32[]{:S(2)}) async-start(s8[5242880]{0:T(1024)(128)(4,1)} %bitcast.123), calls=%async_computation.5 | async-start | bytes 8388608
  112.5 4.2 %slice-start.1 = ((s8[5242880]{0:T(1024)(128)(4,1)}), s8[1048576]{0:T(1024)(128)(4,1)S(1)}, s32[]{:S(2)}) async-start(s8[5242880]{0:T(1024)(128)(4,1)} %bitcast.121), calls=%async_computation.4 | async-start | bytes 2097152
  112.5 4.5 %slice-start.3 = ((s8[5242880]{0:T(1024)(128)(4,1)}), s8[1048576]{0:T(1024)(128)(4,1)S(1)}, s32[]{:S(2)}) async-start(s8[5242880]{0:T(1024)(128)(4,1)} %bitcast.123), calls=%async_computation.6 | async-start | bytes 2097152
  112.9 5.7 %copy-start.2 = (f32[10,32,2048]{2,1,0:T(8,128)}, f32[10,32,2048]{2,1,0:T(8,128)S(1)}, u32[]{:S(2)}) copy-start(f32[10,32,2048]{2,1,0:T(8,128)S(1)} %constant_dynamic-update-slice_fusion.2) | copy-start | bytes 7864324
  117.0 11.5 %copy-start.13 = (s32[16]{0:T(128)S(1)}, s32[16]{0:T(128)}, u32[]{:S(2)}) copy-start(s32[16]{0:T(128)} %get-tuple-element.64) | copy-start | bytes 196
  118.6 36.0 %collective-permute-start.3 = (bf16[32,2048]{1,0:T(8,128)(2,1)S(1)}, bf16[32,2048]{1,0:T(8,128)(2,1)S(1)}, u32[]{:S(2)}, u32[]{:S(2)}) collective-permute-start(bf16[32,2048]{1,0:T(8,128)(2,1)S(1)} %fusion.28), channel_id=1, source_target_pairs={{1,0},{2,1},{3,2},{5,4},{6,5},{7,6},{9,8},{10,9},{11,10},{13,12},{... | collective-permute-start | bytes 393224 | tf_op jit(solution)/shard_map/ppermute | solution.py:21
  119.9 34.7 %collective-permute-start.2 = (bf16[32,2048]{1,0:T(8,128)(2,1)S(1)}, bf16[32,2048]{1,0:T(8,128)(2,1)}, u32[]{:S(2)}, u32[]{:S(2)}) collective-permute-start(bf16[32,2048]{1,0:T(8,128)(2,1)S(1)} %fusion.27), channel_id=1, source_target_pairs={{0,1},{1,2},{2,3},{4,5},{5,6},{6,7},{8,9},{9,10},{10,11},{12,13},{... | collective-permute-start | bytes 393224 | tf_op jit(solution)/shard_map/ppermute | solution.py:19
  137.3 37.7 %all-to-all-start.1 = ((bf16[4,4,32,2048]{3,2,1,0:T(8,128)(2,1)}), bf16[4,4,32,2048]{3,2,1,0:T(8,128)(2,1)}, u32[]{:S(2)}, u32[]{:S(2)}) async-start(bf16[4,4,32,2048]{3,2,1,0:T(8,128)(2,1)} %bitcast.138), calls=%async_computation.1 | async-start | bytes 4194304 | tf_op jit(solution)/shard_map/all_to_all | solution.py:163
  141.8 3.2 %copy-start.17 = (bf16[256]{0:T(256)(128)(2,1)S(1)}, bf16[256]{0:T(256)(128)(2,1)}, u32[]{:S(2)}) copy-start(bf16[256]{0:T(256)(128)(2,1)} %copy-done.16) | copy-start | bytes 1540
  141.8 153.6 %all-reduce.3.cloned.1.call-start = ((), (), s32[]{:S(2)}) async-start(), calls=%async_computation.2 | async-start | bytes 8388608 | tf_op jit(solution)/shard_map/psum | solution.py:184
  149.0 3.6 %copy-start.3 = (f32[10,32,2048]{2,1,0:T(8,128)S(1)}, f32[10,32,2048]{2,1,0:T(8,128)}, u32[]{:S(2)}) copy-start(f32[10,32,2048]{2,1,0:T(8,128)} %copy-done.2) | copy-start | bytes 7864324
  155.7 19.4 %copy-start.12 = (s32[16]{0:T(128)S(1)}, s32[16]{0:T(128)}, u32[]{:S(2)}) copy-start(s32[16]{0:T(128)} %reshape.457) | copy-start | bytes 196
  155.7 19.4 %copy-start.15 = (pred[16]{0:T(512)(128)(4,1)S(1)}, pred[16]{0:T(512)(128)(4,1)}, u32[]{:S(2)}) copy-start(pred[16]{0:T(512)(128)(4,1)} %and.82) | copy-start | bytes 52
  180.3 119.2 %copy-start.1 = (bf16[1024,1024]{1,0:T(8,128)(2,1)S(1)}, bf16[1024,1024]{1,0:T(8,128)(2,1)}, u32[]{:S(2)}) copy-start(bf16[1024,1024]{1,0:T(8,128)(2,1)} %param.21) | copy-start | bytes 6291460
Sparse Core Ops, SparseCore 0:
  149.1 146.2 all-reduce.2
where the time goes:
time: 308 us; the launch traced here: 306 us
  waiting for transfers between devices  126 us (41%)
  local copies, waits for them, and re-layouts  81.2 us (26%)
  matrix products  32.1 us (10%)
  other arithmetic  31.4 us (10%)
  starting transfers between devices  20.8 us (7%)
  between operations  14.5 us (5%)
    psum x1, waiting for transfers between devices, on_device(): summed = lax.psum(weight_part, ('mid', 'off'))  114 us
    all_to_all x1, waiting for transfers between devices, on_device(): lax.all_to_all(outbound.reshape(off_size, capacity, block_rows, 2 * featu...  10.2 us
    ppermute x2, starting transfers between devices, padded(): lax.ppermute(tail, axis, [(i, (i + 1) % count) for i in range(ends)])  9.26 us
    slice x2, local copies, waits for them, and re-layouts, attend(): key_sets[:, :, features:].reshape(blocks, key_count, head_count, head_dim)  8.9 us
    reshape x1, local copies, waits for them, and re-layouts, key_grads(): value_grad.reshape(blocks, key_count, -1)  8.12 us
    reshape x1, local copies, waits for them, and re-layouts, key_grads(): key_grad.reshape(blocks, key_count, -1)  8.09 us
    unnamed x46, local copies, waits for them, and re-layouts  6.28 us
    scatter-add x1, local copies, waits for them, and re-layouts, on_device(): own_grads = own_grads.at[blocks - 1].add(incoming[3 * block_rows:])  6.22 us
  transfers between devices with their start and end apart: 7, of which 3 were waited for; matrix products, arithmetic and copies ran while one was open for 20% of the time, Pallas kernels for 0%

commit v1 on v0

v1 whole, which is shorter than its diff:
```python
import functools

import jax
import jax.numpy as jnp
from jax import lax
from jax.experimental import pallas as pl
from jax.experimental.pallas import tpu as pltpu
from jax.sharding import PartitionSpec as P

HEAD_DIM = 64
BLOCK = 32
GROUP = 4
WIDE = GROUP * HEAD_DIM
VMEM_LIMIT = 56 * 1024 * 1024

NT = (((1,), (1,)), ((), ()))
TN = (((0,), (0,)), ((), ()))


def dot(a, b, dims):
    return lax.dot_general(a, b, dims, preferred_element_type=jnp.float32)


def attend_kernel(
    blocks,
    far_slots,
    slot_total,
    slot_ref,
    live_ref,
    edge_ref,
    query_ref,
    grad_ref,
    mask_ref,
    weight_ref,
    pair_ref,
    edges_in_ref,
    arrived_ref,
    query_grad_ref,
    own_ref,
    edge_out_ref,
    outbound_ref,
    weight_out_ref,
    hit,
    attn,
    attended,
    extended,
    totals,
):
    rows, features = query_ref.shape
    groups = features // WIDE
    stack = GROUP * BLOCK
    keys = (3 + far_slots) * BLOCK
    hit[...] = grad_ref[...] * mask_ref[...]

    @pl.loop(0, groups)
    def _(g):
        cols = pl.ds(pl.multiple_of(g * WIDE, WIDE), WIDE)
        attn[:, cols] = dot(hit[...], weight_ref[cols, :], NT).astype(jnp.bfloat16)

    extended[:BLOCK, :] = edges_in_ref[:BLOCK, :]
    extended[BLOCK : BLOCK + rows, :] = pair_ref[...]
    extended[BLOCK + rows :, :] = edges_in_ref[BLOCK:, :]
    totals[...] = jnp.zeros_like(totals)
    outbound_ref[...] = jnp.zeros_like(outbound_ref)

    row_head = lax.broadcasted_iota(jnp.int32, (stack, WIDE), 0) // BLOCK
    col_head = lax.broadcasted_iota(jnp.int32, (stack, WIDE), 1) // HEAD_DIM
    diagonal = (row_head == col_head).astype(jnp.bfloat16)
    head_of = lax.broadcasted_iota(jnp.int32, (BLOCK, WIDE), 1) // HEAD_DIM
    key_block = lax.broadcasted_iota(jnp.int32, (keys, stack), 0) // BLOCK

    def pick(wide):
        result = wide[:BLOCK]
        for h in range(1, GROUP):
            result = jnp.where(head_of == h, wide[h * BLOCK : (h + 1) * BLOCK], result)
        return result

    @pl.loop(0, blocks)
    def _(n):
        at = pl.ds(pl.multiple_of(n * BLOCK, BLOCK), BLOCK)
        band = pl.ds(pl.multiple_of(n * BLOCK, BLOCK), 3 * BLOCK)
        allowed = jnp.where(key_block == 0, edge_ref[0, n], edge_ref[1, n] * (key_block == 2))
        allowed = jnp.where(key_block == 1, 1, allowed)
        slots = []
        for f in range(far_slots):
            live = live_ref[n, f]
            slots.append(jnp.where(live > 0, slot_ref[n, f], 0))
            allowed = jnp.where(key_block == 3 + f, live, allowed)
        allowed = allowed > 0
        for g in range(groups):
            kc = pl.ds(g * WIDE, WIDE)
            vc = pl.ds(features + g * WIDE, WIDE)
            key = jnp.concatenate(
                [extended[band, kc]] + [arrived_ref[s, :, kc] for s in slots], axis=0
            )
            value = jnp.concatenate(
                [extended[band, vc]] + [arrived_ref[s, :, vc] for s in slots], axis=0
            )
            query = query_ref[at, kc] * jnp.bfloat16(HEAD_DIM**-0.5)
            query = jnp.concatenate([query] * GROUP, axis=0) * diagonal
            grad = jnp.concatenate([attn[at, kc]] * GROUP, axis=0) * diagonal
            scores = jnp.where(allowed, dot(key, query, NT), -jnp.inf)
            powers = jnp.exp(scores - jnp.max(scores, axis=0, keepdims=True))
            prob = powers * (1.0 / jnp.sum(powers, axis=0, keepdims=True))
            half = prob.astype(jnp.bfloat16)
            prob_grad = dot(value, grad, NT)
            row_dot = jnp.sum(prob * prob_grad, axis=0, keepdims=True)
            score_grad = (prob * (prob_grad - row_dot)).astype(jnp.bfloat16)
            attended[at, kc] = pick(dot(half, value, TN)).astype(jnp.bfloat16)
            query_grad_ref[at, kc] = (pick(dot(score_grad, key, TN)) * (HEAD_DIM**-0.5)).astype(
                jnp.bfloat16
            )
            key_grad = jnp.dot(score_grad, query, preferred_element_type=jnp.float32)
            value_grad = jnp.dot(half, grad, preferred_element_type=jnp.float32)
            totals[band, kc] += key_grad[: 3 * BLOCK]
            totals[band, vc] += value_grad[: 3 * BLOCK]
            for f in range(far_slots):
                rows_f = slice((3 + f) * BLOCK, (4 + f) * BLOCK)

                @pl.when(live_ref[n, f] > 0)
                def _(f=f, rows_f=rows_f):
                    outbound_ref[slots[f], :, kc] = key_grad[rows_f].astype(jnp.bfloat16)
                    outbound_ref[slots[f], :, vc] = value_grad[rows_f].astype(jnp.bfloat16)

    own_ref[...] = totals[BLOCK : BLOCK + rows, :]
    edge_out_ref[:BLOCK, :] = totals[:BLOCK, :].astype(jnp.bfloat16)
    edge_out_ref[BLOCK:, :] = totals[BLOCK + rows :, :].astype(jnp.bfloat16)

    for g in range(groups):
        cols = pl.ds(g * WIDE, WIDE)
        weight_out_ref[cols, :] = dot(attended[:, cols], hit[...], TN).astype(jnp.bfloat16)


def gather_kernel(slot_total, chosen_ref, pair_ref, out_ref):
    for s in range(slot_total):
        at = pl.ds(pl.multiple_of(chosen_ref[s] * BLOCK, BLOCK), BLOCK)
        out_ref[s] = pair_ref[at, :]


def finish_kernel(
    slot_total, chosen_ref, filled_ref, own_ref, edge_ref, inbound_ref, key_ref, value_ref, totals
):
    rows, width = own_ref.shape
    features = width // 2
    totals[...] = own_ref[...]
    totals[:BLOCK, :] += edge_ref[:BLOCK, :].astype(jnp.float32)
    totals[rows - BLOCK :, :] += edge_ref[BLOCK:, :].astype(jnp.float32)
    for s in range(slot_total):

        @pl.when(filled_ref[s] > 0)
        def _(s=s):
            at = pl.ds(pl.multiple_of(chosen_ref[s] * BLOCK, BLOCK), BLOCK)
            totals[at, :] += inbound_ref[s].astype(jnp.float32)

    key_ref[...] = totals[:, :features].astype(jnp.bfloat16)
    value_ref[...] = totals[:, features:].astype(jnp.bfloat16)


SMEM = pl.BlockSpec(memory_space=pltpu.SMEM)
VMEM = pl.BlockSpec(memory_space=pltpu.VMEM)


def edge_swap(head, tail):
    count = lax.axis_size("off")
    before = lax.ppermute(tail, "off", [(i, i + 1) for i in range(count - 1)])
    after = lax.ppermute(head, "off", [(i + 1, i) for i in range(count - 1)])
    return before, after


def on_device(query_rows, key_rows, value_rows, grad_out, out_weight, masked_rows, far_blocks):
    off_size = lax.axis_size("off")
    mid_size = lax.axis_size("mid")
    position = lax.axis_index("off")
    row_count, features = query_rows.shape
    width = 2 * features
    blocks = row_count // BLOCK
    far_slots = far_blocks.shape[1]
    capacity = max(2, -(-(blocks * far_slots) // off_size))
    slot_total = off_size * capacity
    total_blocks = blocks * off_size

    far_table = far_blocks.reshape(off_size, blocks * far_slots)
    live_all = far_table >= 0
    owner_all = jnp.where(live_all, far_table // blocks, -1)
    owner_hits = (owner_all[:, :, None] == jnp.arange(off_size)[None, None, :]).astype(jnp.int32)
    rank_all = jnp.sum((jnp.cumsum(owner_hits, axis=1) - owner_hits) * owner_hits, axis=2)
    mine_live = lax.dynamic_index_in_dim(live_all, position, 0, keepdims=False)
    mine_owner = lax.dynamic_index_in_dim(owner_all, position, 0, keepdims=False)
    mine_rank = lax.dynamic_index_in_dim(rank_all, position, 0, keepdims=False)
    mine_slot = jnp.where(mine_live, mine_owner * capacity + mine_rank, 0)
    wanted = live_all & (owner_all == position)
    matches = wanted[:, :, None] & (rank_all[:, :, None] == jnp.arange(capacity)[None, None, :])
    local_ids = far_table - position * blocks
    chosen = jnp.sum(jnp.where(matches, local_ids[:, :, None], 0), axis=1).reshape(-1)
    filled = jnp.any(matches, axis=1).reshape(-1).astype(jnp.int32)
    global_block = position * blocks + jnp.arange(blocks)
    edge_ok = jnp.stack([global_block >= 1, global_block <= total_blocks - 2]).astype(jnp.int32)

    pair_rows = jnp.concatenate([key_rows, value_rows], axis=1)
    before, after = edge_swap(pair_rows[:BLOCK], pair_rows[row_count - BLOCK :])
    outgoing = pl.pallas_call(
        functools.partial(gather_kernel, slot_total),
        out_shape=jax.ShapeDtypeStruct((slot_total, BLOCK, width), jnp.bfloat16),
        in_specs=[SMEM, VMEM],
        out_specs=VMEM,
        compiler_params=pltpu.CompilerParams(vmem_limit_bytes=VMEM_LIMIT),
    )(chosen, pair_rows)

    def exchange(parts):
        parts = parts.reshape(off_size, capacity, BLOCK, width)
        parts = lax.all_to_all(parts, "off", split_axis=0, concat_axis=0, tiled=True)
        return parts.reshape(slot_total, BLOCK, width)

    arrived = exchange(outgoing)
    query_grad, own, edges, outbound, weight_part = pl.pallas_call(
        functools.partial(attend_kernel, blocks, far_slots, slot_total),
        out_shape=(
            jax.ShapeDtypeStruct((row_count, features), jnp.bfloat16),
            jax.ShapeDtypeStruct((row_count, width), jnp.float32),
            jax.ShapeDtypeStruct((2 * BLOCK, width), jnp.bfloat16),
            jax.ShapeDtypeStruct((slot_total, BLOCK, width), jnp.bfloat16),
            jax.ShapeDtypeStruct((features, features), jnp.bfloat16),
        ),
        in_specs=[SMEM] * 3 + [VMEM] * 7,
        out_specs=(VMEM,) * 5,
        scratch_shapes=[
            pltpu.VMEM((row_count, features), jnp.bfloat16),
            pltpu.VMEM((row_count, features), jnp.bfloat16),
            pltpu.VMEM((row_count, features), jnp.bfloat16),
            pltpu.VMEM((row_count + 2 * BLOCK, width), jnp.bfloat16),
            pltpu.VMEM((row_count + 2 * BLOCK, width), jnp.float32),
        ],
        compiler_params=pltpu.CompilerParams(vmem_limit_bytes=VMEM_LIMIT),
    )(
        mine_slot.reshape(blocks, far_slots).astype(jnp.int32),
        mine_live.reshape(blocks, far_slots).astype(jnp.int32),
        edge_ok,
        query_rows,
        grad_out,
        masked_rows[:, None].astype(jnp.bfloat16),
        out_weight,
        pair_rows,
        jnp.concatenate([before, after], axis=0),
        arrived,
    )
    inbound = exchange(outbound)
    before, after = edge_swap(edges[:BLOCK], edges[BLOCK:])
    weight_scale = (row_count * mid_size * off_size) ** (-0.5)
    summed = lax.psum(weight_part, ("mid", "off"))
    weight_grad = (summed.astype(jnp.float32) * weight_scale).astype(jnp.bfloat16)
    key_grad, value_grad = pl.pallas_call(
        functools.partial(finish_kernel, slot_total),
        out_shape=(jax.ShapeDtypeStruct((row_count, features), jnp.bfloat16),) * 2,
        in_specs=[SMEM, SMEM, VMEM, VMEM, VMEM],
        out_specs=(VMEM,) * 2,
        scratch_shapes=[pltpu.VMEM((row_count, width), jnp.float32)],
        compiler_params=pltpu.CompilerParams(vmem_limit_bytes=VMEM_LIMIT),
    )(chosen, filled, own, jnp.concatenate([before, after], axis=0), inbound)
    return query_grad, key_grad, value_grad, weight_grad


def solution(mesh):
    rows = P(("mid", "off"), None)
    return jax.shard_map(
        on_device,
        mesh=mesh,
        in_specs=(rows, rows, rows, rows, P(), P(("mid", "off")), P()),
        out_specs=(rows, rows, rows, P()),
        check_vma=False,
    )
```

time: 308 us -> 235 us (0.76)
  local copies, waits for them, and re-layouts: 81.2 us -> 11.1 us
  Pallas kernels: 0 us -> 32.3 us
  matrix products: 32.1 us -> 0 us
  waiting for transfers between devices: 126 us -> 154 us
  other arithmetic: 31.4 us -> 6.13 us
  starting transfers between devices: 20.8 us -> 16.8 us
    pallas_call x0 -> x3, Pallas kernels: none -> 32.3 us  [the longest x1 25.7 us: on_device(): pl.pallas_call(functools.partial(attend_kernel, blocks, far_slots, slot_t...]
    dot_general x9 -> x0, matrix products: 32.1 us -> none  [the longest x1 4.63 us: on_device(): jnp.einsum('ns,sx->nx', selector, inbound, preferred_element_type=jnp.flo...]
    reshape x8 -> x0, local copies, waits for them, and re-layouts: 24.3 us -> none  [the longest x1 8.12 us: key_grads(): value_grad.reshape(blocks, key_count, -1)]
    psum x1, waiting for transfers between devices: 114 us -> 134 us  [on_device(): summed = lax.psum(weight_part, ('mid', 'off'))]
    slice x7 -> x2, local copies, waits for them, and re-layouts: 19.2 us -> 1 us  [the longest x1 0.98 us: on_device(): before, after = edge_swap(pair_rows[:BLOCK], pair_rows[row_count - BLOCK:])]
    concatenate x4 -> x2, other arithmetic: 11.1 us -> 1.46 us  [on_device(): jnp.concatenate([before, after], axis=0)]
    scatter-add x4 -> x0, local copies, waits for them, and re-layouts: 9.17 us -> none  [the longest x1 6.22 us: on_device(): own_grads = own_grads.at[blocks - 1].add(incoming[3 * block_rows:])]
    select_n x5 -> x0, other arithmetic: 6.9 us -> none  [the longest x1 3.21 us: on_device(): jnp.where(filled[:, None, None], outgoing, jnp.zeros((), jnp.bfloat16))]
  transfers between devices with their start and end apart: 7 -> 7, of which waited for: 3 -> 4; matrix products, arithmetic and copies ran while one was open for 20% -> 4% of each run, Pallas kernels for 0% -> 0%
where the time goes in v1:
time: 235 us
  waiting for transfers between devices  154 us (66%)
  Pallas kernels  32.3 us (14%)
  starting transfers between devices  16.8 us (7%)
  between operations  14.1 us (6%)
  local copies, waits for them, and re-layouts  11.1 us (5%)
  other arithmetic  6.13 us (3%)
    psum x1, waiting for transfers between devices, on_device(): summed = lax.psum(weight_part, ('mid', 'off'))  134 us
    pallas_call x1, Pallas kernels, on_device(): pl.pallas_call(functools.partial(attend_kernel, blocks, far_slots, slot_t...  25.7 us
    all_to_all x2, waiting for transfers between devices, exchange(): lax.all_to_all(parts, 'off', split_axis=0, concat_axis=0, tiled=True)  16.9 us
    all_to_all x2, starting transfers between devices, exchange(): lax.all_to_all(parts, 'off', split_axis=0, concat_axis=0, tiled=True)  8.13 us
    ppermute x2, starting transfers between devices, edge_swap(): before = lax.ppermute(tail, 'off', [(i, i + 1) for i in range(count - 1)])  6.13 us
    unnamed x12, local copies, waits for them, and re-layouts  5.69 us
  transfers between devices with their start and end apart: 7, of which 4 were waited for; matrix products, arithmetic and copies ran while one was open for 4% of the time, Pallas kernels for 0%

profile of v1, /device:TPU:0, one launch (start us, length us, event | category | flops | bytes accessed | tf_op | source)
XLA Modules:
  0.0 234.6 jit_solution(12968769725435621159)
XLA Ops:
  7.2 0.8 copy.12
  7.9 0.1 reshape.109
  8.0 0.1 fusion
  8.2 0.2 select_reduce_fusion.1
  8.4 0.1 select_reduce_fusion
  8.5 0.6 reshape.110.chosen_ref
  9.1 1.1 constant_dynamic-update-slice_fusion.1
  10.2 1.1 constant_dynamic-update-slice_fusion.pair_ref
  11.2 0.0 copy-start.2
  11.2 1.0 copy-done.2
  12.2 2.7 %shard_map.102 = bf16[16,32,2048]{2,1,0:T(8,128)(2,1)} custom-call(s32[16]{0:T(128)} %reshape.110.chosen_ref, bf16[256,2048]{1,0:T(8,128)(2,1)} %copy-done.2), custom_call_target="tpu_custom_call" | custom-call | tf_op jit(solution)/shard_map/pallas_call | solution.py:201
  14.9 0.0 copy-start.4
  14.9 4.4 %all-to-all-start = ((bf16[4,4,32,2048]{3,2,1,0:T(8,128)(2,1)}), bf16[4,4,32,2048]{3,2,1,0:T(8,128)(2,1)S(1)}, u32[]{:S(2)}, u32[]{:S(2)}) async-start(bf16[4,4,32,2048]{3,2,1,0:T(8,128)(2,1)} %bitcast.5), calls=%async_computation | async-start | bytes 4194304 | tf_op jit(solution)/shard_map/all_to_all | solution.py:211
  19.3 1.0 fusion.13
  20.3 2.4 %collective-permute-start = (bf16[32,2048]{1,0:T(8,128)(2,1)S(1)}, bf16[32,2048]{1,0:T(8,128)(2,1)S(1)}, u32[]{:S(2)}, u32[]{:S(2)}) collective-permute-start(bf16[32,2048]{1,0:T(8,128)(2,1)S(1)} %get-tuple-element.23), channel_id=1, source_target_pairs={{0,1},{1,2},{2,3},{4,5},{5,6},{6,7},{8,9},{9,10},{10,11},{12,13},{... | collective-permute-start | bytes 393224 | tf_op jit(solution)/shard_map/ppermute | solution.py:165
  22.7 1.3 collective-permute-start.1
  24.0 0.0 copy-done.4
  24.1 0.7 reshape.115.live_ref
  24.8 0.7 select_n.46.slot_ref
  25.4 0.7 convert_element_type.39.mask_ref
  26.2 0.6 add_convert_fusion.edge_ref
  26.7 0.0 collective-permute-done
  26.7 0.7 collective-permute-done.1
  27.4 0.7 pad_maximum_fusion.edges_in_ref
  28.1 16.9 %all-to-all-done = bf16[4,4,32,2048]{3,2,1,0:T(8,128)(2,1)S(1)} async-done(((bf16[4,4,32,2048]{3,2,1,0:T(8,128)(2,1)}), bf16[4,4,32,2048]{3,2,1,0:T(8,128)(2,1)S(1)}, u32[]{:S(2)}, u32[]{:S(2)}) %all-to-all-start) | async-done | bytes 2097184 | tf_op jit(solution)/shard_map/all_to_all | solution.py:211
  45.0 0.0 copy-start.1
  45.0 1.3 copy-done.1
  46.3 25.7 %shard_map.103 = (bf16[256,1024]{1,0:T(8,128)(2,1)}, f32[256,2048]{1,0:T(8,128)}, bf16[64,2048]{1,0:T(8,128)(2,1)}, bf16[16,32,2048]{2,1,0:T(8,128)(2,1)}, bf16[1024,1024]{1,0:T(8,128)(2,1)}) custom-call(s32[8,2]{1,0:T(8,128)} %select_n.46.slot_ref, s32[8,2]{1,0:T(8,128)} %reshape.115.live_ref, s32[2,8]{1,0:T(2,128)} %add_convert_fusion.edge_ref, ...), custom_call_target="tpu_custom_call" | custom-call | tf_op jit(solution)/shard_map/pallas_call | solution.py:215
  72.0 3.8 %all-to-all-start.1 = ((bf16[4,4,32,2048]{3,2,1,0:T(8,128)(2,1)}), bf16[4,4,32,2048]{3,2,1,0:T(8,128)(2,1)S(1)}, u32[]{:S(2)}, u32[]{:S(2)}) async-start(bf16[4,4,32,2048]{3,2,1,0:T(8,128)(2,1)} %bitcast.7), calls=%async_computation.1 | async-start | bytes 4194304 | tf_op jit(solution)/shard_map/all_to_all | solution.py:211
  75.8 0.0 copy-start.3
  75.8 0.0 all-reduce.2.cloned.1.call-start
  75.8 0.7 all-reduce.2.cloned.1.call-update
  76.5 0.2 copy-done.3
  76.7 3.7 %collective-permute-start.2 = (bf16[32,2048]{1,0:T(8,128)(2,1)S(1)}, bf16[32,2048]{1,0:T(8,128)(2,1)S(1)}, u32[]{:S(2)}, u32[]{:S(2)}) collective-permute-start(bf16[32,2048]{1,0:T(8,128)(2,1)S(1)} %get-tuple-element.25), channel_id=1, source_target_pairs={{0,1},{1,2},{2,3},{4,5},{5,6},{6,7},{8,9},{9,10},{10,11},{12,13},{... | collective-permute-start | bytes 393224 | tf_op jit(solution)/shard_map/ppermute | solution.py:165
  80.4 1.3 collective-permute-start.3
  81.7 0.1 fusion.2
  81.9 0.6 reshape.116.filled_ref
  82.5 0.0 collective-permute-done.2
  82.5 1.4 collective-permute-done.3
  83.8 0.7 pad_maximum_fusion.1.edge_ref
  84.6 134.4 %all-reduce.2.cloned.1.call-done = bf16[1024,1024]{1,0:T(8,128)(2,1)} async-done(((bf16[1024,1024]{1,0:T(8,128)(2,1)}), bf16[1024,1024]{1,0:T(8,128)(2,1)}) %all-reduce.2.cloned.1.call-update) | async-done | bytes 2097168 | tf_op jit(solution)/shard_map/psum | solution.py:249
  219.0 3.5 %multiply_convert_fusion = bf16[1024,1024]{1,0:T(8,128)(2,1)} fusion(bf16[1024,1024]{1,0:T(8,128)(2,1)} %all-reduce.2.cloned.1.call-done), kind=kLoop, calls=%fused_computation | loop fusion | flops 3145728 | bytes 4194304 | tf_op jit(solution)/shard_map/convert_element_type | solution.py:250
  222.5 0.0 all-to-all-done.1
  222.5 0.0 copy-start
  222.5 1.3 copy-done
  223.8 4.0 %shard_map.104 = (bf16[256,1024]{1,0:T(8,128)(2,1)}, bf16[256,1024]{1,0:T(8,128)(2,1)}) custom-call(s32[16]{0:T(128)} %reshape.110.chosen_ref, s32[16]{0:T(128)} %reshape.116.filled_ref, f32[256,2048]{1,0:T(8,128)} %get-tuple-element.12.own_ref, bf16[64,2048]{1,0:T(8,128)(2,1)} %pad_maximum_fusion.1.edge_ref, bf16[16,32,2048]{2,1,0:T(8,128)(2,1)} %bitcast.4), custom_call_target="tpu_custom_call" | custom-call | tf_op jit(solution)/shard_map/pallas_call | solution.py:251
  (8 shorter events, 0.1 us)
Async XLA Ops:
  11.2 1.0 copy-start.2
  14.9 9.1 %copy-start.4 = (s32[256]{0:T(256)S(1)}, s32[256]{0:T(256)}, u32[]{:S(2)}) copy-start(s32[256]{0:T(256)} %param.12) | copy-start | bytes 3076
  14.9 30.1 %all-to-all-start = ((bf16[4,4,32,2048]{3,2,1,0:T(8,128)(2,1)}), bf16[4,4,32,2048]{3,2,1,0:T(8,128)(2,1)S(1)}, u32[]{:S(2)}, u32[]{:S(2)}) async-start(bf16[4,4,32,2048]{3,2,1,0:T(8,128)(2,1)} %bitcast.5), calls=%async_computation | async-start | bytes 4194304 | tf_op jit(solution)/shard_map/all_to_all | solution.py:211
  20.3 6.4 %collective-permute-start = (bf16[32,2048]{1,0:T(8,128)(2,1)S(1)}, bf16[32,2048]{1,0:T(8,128)(2,1)S(1)}, u32[]{:S(2)}, u32[]{:S(2)}) collective-permute-start(bf16[32,2048]{1,0:T(8,128)(2,1)S(1)} %get-tuple-element.23), channel_id=1, source_target_pairs={{0,1},{1,2},{2,3},{4,5},{5,6},{6,7},{8,9},{9,10},{10,11},{12,13},{... | collective-permute-start | bytes 393224 | tf_op jit(solution)/shard_map/ppermute | solution.py:165
  22.7 4.7 %collective-permute-start.1 = (bf16[32,2048]{1,0:T(8,128)(2,1)S(1)}, bf16[32,2048]{1,0:T(8,128)(2,1)S(1)}, u32[]{:S(2)}, u32[]{:S(2)}) collective-permute-start(bf16[32,2048]{1,0:T(8,128)(2,1)S(1)} %get-tuple-element.24), channel_id=1, source_target_pairs={{1,0},{2,1},{3,2},{5,4},{6,5},{7,6},{9,8},{10,9},{11,10},{13,12},{... | collective-permute-start | bytes 393224 | tf_op jit(solution)/shard_map/ppermute | solution.py:166
  45.0 1.3 copy-start.1
  72.0 150.5 %all-to-all-start.1 = ((bf16[4,4,32,2048]{3,2,1,0:T(8,128)(2,1)}), bf16[4,4,32,2048]{3,2,1,0:T(8,128)(2,1)S(1)}, u32[]{:S(2)}, u32[]{:S(2)}) async-start(bf16[4,4,32,2048]{3,2,1,0:T(8,128)(2,1)} %bitcast.7), calls=%async_computation.1 | async-start | bytes 4194304 | tf_op jit(solution)/shard_map/all_to_all | solution.py:211
  75.8 0.9 copy-start.3
  75.8 143.3 %all-reduce.2.cloned.1.call-start = ((), (), s32[]{:S(2)}) async-start(), calls=%async_computation.2 | async-start | bytes 4194304 | tf_op jit(solution)/shard_map/psum | solution.py:249
  76.7 5.7 %collective-permute-start.2 = (bf16[32,2048]{1,0:T(8,128)(2,1)S(1)}, bf16[32,2048]{1,0:T(8,128)(2,1)S(1)}, u32[]{:S(2)}, u32[]{:S(2)}) collective-permute-start(bf16[32,2048]{1,0:T(8,128)(2,1)S(1)} %get-tuple-element.25), channel_id=1, source_target_pairs={{0,1},{1,2},{2,3},{4,5},{5,6},{6,7},{8,9},{9,10},{10,11},{12,13},{... | collective-permute-start | bytes 393224 | tf_op jit(solution)/shard_map/ppermute | solution.py:165
  80.4 3.4 %collective-permute-start.3 = (bf16[32,2048]{1,0:T(8,128)(2,1)S(1)}, bf16[32,2048]{1,0:T(8,128)(2,1)S(1)}, u32[]{:S(2)}, u32[]{:S(2)}) collective-permute-start(bf16[32,2048]{1,0:T(8,128)(2,1)S(1)} %get-tuple-element.26), channel_id=1, source_target_pairs={{1,0},{2,1},{3,2},{5,4},{6,5},{7,6},{9,8},{10,9},{11,10},{13,12},{... | collective-permute-start | bytes 393224 | tf_op jit(solution)/shard_map/ppermute | solution.py:166
  222.5 1.3 copy-start
Sparse Core Ops, SparseCore 0:
  81.9 137.0 all-reduce.1

commit v2 on v1

--- a/solution.py
+++ b/solution.py
@@ -160,6 +160,126 @@
 VMEM = pl.BlockSpec(memory_space=pltpu.VMEM)
 
 
+def bits_of(count):
+    return [1 << i for i in range(count.bit_length() - 1)]
+
+
+def chain_orders(mid_size, off_size):
+    off_bits = [("off", b) for b in bits_of(off_size)]
+    mid_bits = [("mid", b) for b in bits_of(mid_size)]
+    first = off_bits[:1] + mid_bits + off_bits[1:]
+    second = off_bits[:1] + mid_bits[1:2] + mid_bits[:1] + mid_bits[2:] + off_bits[1:]
+    return first, second
+
+
+def weight_sum_kernel(orders, scale, part_ref, out_ref, held, landed, whole, send_sem, recv_sem):
+    pieces = part_ref.shape[0]
+    steps = len(orders[0])
+    span = pieces // 2
+    place = {"mid": lax.axis_index("mid"), "off": lax.axis_index("off")}
+
+    def bit_of(axis, bit):
+        return (place[axis] // bit) % 2
+
+    def partner(axis, bit):
+        other = place[axis] + bit - 2 * bit * bit_of(axis, bit)
+        return (other, place["off"]) if axis == "mid" else (place["mid"], other)
+
+    barrier = pltpu.get_barrier_semaphore()
+    for axis, bit in orders[0]:
+        pl.semaphore_signal(
+            barrier, inc=1, device_id=partner(axis, bit), device_id_type=pl.DeviceIdType.MESH
+        )
+    held[...] = part_ref[...]
+    pl.semaphore_wait(barrier, steps)
+
+    starts = [[None] * (steps + 1) for _ in orders]
+    for c, order in enumerate(orders):
+        starts[c][0] = c * span
+        for i, (axis, bit) in enumerate(order):
+            starts[c][i + 1] = starts[c][i] + bit_of(axis, bit) * (span >> (i + 1))
+
+    def remote(src, dst, c, k, axis, bit):
+        return pltpu.make_async_remote_copy(
+            src_ref=src,
+            dst_ref=dst,
+            send_sem=send_sem.at[c, k],
+            recv_sem=recv_sem.at[c, k],
+            device_id=partner(axis, bit),
+            device_id_type=pl.DeviceIdType.MESH,
+        )
+
+    def halve(c, i):
+        axis, bit = orders[c][i]
+        size = span >> (i + 1)
+        give = starts[c][i] + (1 - bit_of(axis, bit)) * size
+        room = c * span + span - 2 * size
+        return remote(
+            held.at[pl.ds(give, size)], landed.at[pl.ds(room, size)], c, i, axis, bit
+        )
+
+    def double(c, i):
+        axis, bit = orders[c][i]
+        size = span >> (i + 1)
+        mine = whole.at[pl.ds(starts[c][i + 1], size)]
+        return remote(mine, mine, c, steps + i, axis, bit)
+
+    copies = [halve(c, 0) for c in range(2)]
+    for copy in copies:
+        copy.start()
+    for i in range(steps):
+        size = span >> (i + 1)
+        for c in range(2):
+            copies[c].wait()
+            at = pl.ds(starts[c][i + 1], size)
+            room = c * span + span - 2 * size
+            total = held[at].astype(jnp.float32) + landed[room : room + size].astype(jnp.float32)
+            if i + 1 < steps:
+                held[at] = total.astype(jnp.bfloat16)
+                copies[c] = halve(c, i + 1)
+            else:
+                whole[at] = (total * scale).astype(jnp.bfloat16)
+                copies[c] = double(c, i)
+            copies[c].start()
+    for i in reversed(range(steps)):
+        for c in range(2):
+            copies[c].wait()
+            if i > 0:
+                copies[c] = double(c, i - 1)
+                copies[c].start()
+    out_ref[...] = whole[...]
+
+
+def weight_sum(part, mid_size, off_size, scale):
+    rows, columns = part.shape
+    orders = chain_orders(mid_size, off_size)
+    steps = len(orders[0])
+    splits = max(1, 32 * mid_size * off_size // rows)
+    pieces, wide = splits * rows // 16, columns // splits
+    part = part.reshape(rows // 16, 16, splits, wide).transpose(2, 0, 1, 3)
+    total = pl.pallas_call(
+        functools.partial(weight_sum_kernel, orders, scale),
+        out_shape=jax.ShapeDtypeStruct((pieces, 16, wide), jnp.bfloat16),
+        in_specs=[VMEM],
+        out_specs=VMEM,
+        scratch_shapes=[
+            pltpu.VMEM((pieces, 16, wide), jnp.bfloat16),
+            pltpu.VMEM((pieces, 16, wide), jnp.bfloat16),
+            pltpu.VMEM((pieces, 16, wide), jnp.bfloat16),
+            pltpu.SemaphoreType.DMA((2, 2 * steps)),
+            pltpu.SemaphoreType.DMA((2, 2 * steps)),
+        ],
+        compiler_params=pltpu.CompilerParams(
+            vmem_limit_bytes=16 * 1024 * 1024, collective_id=0, has_side_effects=True
+        ),
+        cost_estimate=pl.CostEstimate(
+            flops=2 * rows * columns, bytes_accessed=64 * rows * columns, transcendentals=0
+        ),
+    )(part.reshape(pieces, 16, wide))
+    total = total.reshape(splits, rows // 16, 16, wide).transpose(1, 2, 0, 3)
+    return total.reshape(rows, columns)
+
+
 def edge_swap(head, tail):
     count = lax.axis_size("off")
     before = lax.ppermute(tail, "off", [(i, i + 1) for i in range(count - 1)])
@@ -246,8 +366,7 @@
     inbound = exchange(outbound)
     before, after = edge_swap(edges[:BLOCK], edges[BLOCK:])
     weight_scale = (row_count * mid_size * off_size) ** (-0.5)
-    summed = lax.psum(weight_part, ("mid", "off"))
-    weight_grad = (summed.astype(jnp.float32) * weight_scale).astype(jnp.bfloat16)
+    weight_grad = weight_sum(weight_part, mid_size, off_size, weight_scale)
     key_grad, value_grad = pl.pallas_call(
         functools.partial(finish_kernel, slot_total),
         out_shape=(jax.ShapeDtypeStruct((row_count, features), jnp.bfloat16),) * 2,

time: 235 us -> 133 us (0.57)
  waiting for transfers between devices: 154 us -> 17.6 us
  Pallas kernels: 32.3 us -> 81 us
  between operations: 14.1 us -> 0.79 us
  other arithmetic: 6.13 us -> 2.63 us
    psum x1 -> x0, waiting for transfers between devices: 134 us -> none  [on_device(): summed = lax.psum(weight_part, ('mid', 'off'))]
    pallas_call x0 -> x1, Pallas kernels: none -> 48.6 us  [weight_sum(): pl.pallas_call(functools.partial(weight_sum_kernel, orders, scale), out_s...]
    convert_element_type x1 -> x0, other arithmetic: 3.48 us -> none  [on_device(): (summed.astype(jnp.float32) * weight_scale).astype(jnp.bfloat16)]
    unnamed x12 -> x13, local copies, waits for them, and re-layouts: 5.69 us -> 7.07 us
  transfers between devices with their start and end apart: 7 -> 6, of which waited for: 4 -> 2; matrix products, arithmetic and copies ran while one was open for 4% -> 4% of each run, Pallas kernels for 0% -> 37%
where the time goes in v2:
time: 133 us; the launch traced here: 132 us
  Pallas kernels  81 us (61%)
  starting transfers between devices  17.8 us (13%)
  waiting for transfers between devices  17.6 us (13%)
  local copies, waits for them, and re-layouts  12.5 us (9%)
  other arithmetic  2.63 us (2%)
    pallas_call x1, Pallas kernels, weight_sum(): pl.pallas_call(functools.partial(weight_sum_kernel, orders, scale), out_s...  48.6 us
    pallas_call x1, Pallas kernels, on_device(): pl.pallas_call(functools.partial(attend_kernel, blocks, far_slots, slot_t...  25.7 us
    all_to_all x2, waiting for transfers between devices, exchange(): lax.all_to_all(parts, 'off', split_axis=0, concat_axis=0, tiled=True)  16.9 us
    all_to_all x2, starting transfers between devices, exchange(): lax.all_to_all(parts, 'off', split_axis=0, concat_axis=0, tiled=True)  8.95 us
    unnamed x13, local copies, waits for them, and re-layouts  7.07 us
    ppermute x2, starting transfers between devices, edge_swap(): before = lax.ppermute(tail, 'off', [(i, i + 1) for i in range(count - 1)])  6.25 us
    pallas_call x1, Pallas kernels, on_device(): pl.pallas_call(functools.partial(finish_kernel, slot_total), out_shape=(j...  3.96 us
    pallas_call x1, Pallas kernels, on_device(): pl.pallas_call(functools.partial(gather_kernel, slot_total), out_shape=ja...  2.69 us
  transfers between devices with their start and end apart: 6, of which 2 were waited for; matrix products, arithmetic and copies ran while one was open for 4% of the time, Pallas kernels for 37%

profile of v2, /device:TPU:0, one launch (start us, length us, event | category | flops | bytes accessed | tf_op | source)
XLA Modules:
  0.0 132.2 jit_solution(633556319138252053)
XLA Ops:
  0.6 0.8 copy.12
  1.4 0.1 reshape.109
  1.5 0.1 fusion
  1.6 0.2 select_reduce_fusion.1
  1.8 0.1 select_reduce_fusion
  2.0 0.6 reshape.110.chosen_ref
  2.6 1.1 constant_dynamic-update-slice_fusion.1
  3.7 1.1 constant_dynamic-update-slice_fusion.pair_ref
  4.7 0.0 copy-start.2
  4.8 1.0 copy-done.2
  5.7 2.7 %shard_map.102 = bf16[16,32,2048]{2,1,0:T(8,128)(2,1)} custom-call(s32[16]{0:T(128)} %reshape.110.chosen_ref, bf16[256,2048]{1,0:T(8,128)(2,1)} %copy-done.2), custom_call_target="tpu_custom_call" | custom-call | tf_op jit(solution)/shard_map/pallas_call | solution.py:321
  8.4 0.0 copy-start.4
  8.4 4.4 %all-to-all-start = ((bf16[4,4,32,2048]{3,2,1,0:T(8,128)(2,1)}), bf16[4,4,32,2048]{3,2,1,0:T(8,128)(2,1)S(1)}, u32[]{:S(2)}, u32[]{:S(2)}) async-start(bf16[4,4,32,2048]{3,2,1,0:T(8,128)(2,1)} %bitcast.8), calls=%async_computation | async-start | bytes 4194304 | tf_op jit(solution)/shard_map/all_to_all | solution.py:331
  12.8 1.0 fusion.13
  13.8 2.4 %collective-permute-start = (bf16[32,2048]{1,0:T(8,128)(2,1)S(1)}, bf16[32,2048]{1,0:T(8,128)(2,1)S(1)}, u32[]{:S(2)}, u32[]{:S(2)}) collective-permute-start(bf16[32,2048]{1,0:T(8,128)(2,1)S(1)} %get-tuple-element.23), channel_id=1, source_target_pairs={{0,1},{1,2},{2,3},{4,5},{5,6},{6,7},{8,9},{9,10},{10,11},{12,13},{... | collective-permute-start | bytes 393224 | tf_op jit(solution)/shard_map/ppermute | solution.py:285
  16.2 1.3 collective-permute-start.1
  17.5 0.0 copy-done.4
  17.6 0.7 reshape.115.live_ref
  18.3 0.7 select_n.46.slot_ref
  18.9 0.7 convert_element_type.31.mask_ref
  19.7 0.6 add_convert_fusion.edge_ref
  20.2 0.0 collective-permute-done
  20.2 0.7 collective-permute-done.1
  20.9 0.7 pad_maximum_fusion.edges_in_ref
  21.6 16.9 %all-to-all-done = bf16[4,4,32,2048]{3,2,1,0:T(8,128)(2,1)S(1)} async-done(((bf16[4,4,32,2048]{3,2,1,0:T(8,128)(2,1)}), bf16[4,4,32,2048]{3,2,1,0:T(8,128)(2,1)S(1)}, u32[]{:S(2)}, u32[]{:S(2)}) %all-to-all-start) | async-done | bytes 2097184 | tf_op jit(solution)/shard_map/all_to_all | solution.py:331
  38.5 0.0 copy-start.1
  38.5 1.3 copy-done.1
  39.8 25.7 %shard_map.103 = (bf16[256,1024]{1,0:T(8,128)(2,1)}, f32[256,2048]{1,0:T(8,128)}, bf16[64,2048]{1,0:T(8,128)(2,1)}, bf16[16,32,2048]{2,1,0:T(8,128)(2,1)}, bf16[1024,1024]{1,0:T(8,128)(2,1)}) custom-call(s32[8,2]{1,0:T(8,128)} %select_n.46.slot_ref, s32[8,2]{1,0:T(8,128)} %reshape.115.live_ref, s32[2,8]{1,0:T(2,128)} %add_convert_fusion.edge_ref, ...), custom_call_target="tpu_custom_call" | custom-call | tf_op jit(solution)/shard_map/pallas_call | solution.py:335
  65.5 0.0 copy-start.3
  65.5 4.6 %all-to-all-start.1 = ((bf16[4,4,32,2048]{3,2,1,0:T(8,128)(2,1)}), bf16[4,4,32,2048]{3,2,1,0:T(8,128)(2,1)}, u32[]{:S(2)}, u32[]{:S(2)}) async-start(bf16[4,4,32,2048]{3,2,1,0:T(8,128)(2,1)} %bitcast.10), calls=%async_computation.1 | async-start | bytes 4194304 | tf_op jit(solution)/shard_map/all_to_all | solution.py:331
  70.1 0.0 copy-done.3
  70.1 3.8 %collective-permute-start.2 = (bf16[32,2048]{1,0:T(8,128)(2,1)S(1)}, bf16[32,2048]{1,0:T(8,128)(2,1)S(1)}, u32[]{:S(2)}, u32[]{:S(2)}) collective-permute-start(bf16[32,2048]{1,0:T(8,128)(2,1)S(1)} %get-tuple-element.25), channel_id=1, source_target_pairs={{0,1},{1,2},{2,3},{4,5},{5,6},{6,7},{8,9},{9,10},{10,11},{12,13},{... | collective-permute-start | bytes 393224 | tf_op jit(solution)/shard_map/ppermute | solution.py:285
  74.0 1.3 collective-permute-start.3
  75.3 0.1 fusion.2
  75.4 0.6 reshape.116.filled_ref
  75.9 0.0 copy-start
  76.0 1.6 %copy-done = bf16[1024,1024]{1,0:T(8,128)(2,1)S(1)} copy-done((bf16[1024,1024]{1,0:T(8,128)(2,1)S(1)}, bf16[1024,1024]{1,0:T(8,128)(2,1)}, u32[]{:S(2)}) %copy-start) | copy-done | bytes 2097176
  77.5 48.6 %shard_map.105 = bf16[64,16,1024]{2,1,0:T(8,128)(2,1)S(1)} custom-call(bf16[64,16,1024]{2,1,0:T(8,128)(2,1)S(1)} %bitcast.7), custom_call_target="tpu_custom_call" | custom-call | flops 2097152 | bytes 67108864 | tf_op jit(solution)/shard_map/pallas_call | solution.py:260
  126.2 0.0 collective-permute-done.2
  126.2 0.0 collective-permute-done.3
  126.2 0.7 pad_maximum_fusion.1.edge_ref
  126.9 0.0 all-to-all-done.1
  126.9 4.0 %shard_map.104 = (bf16[256,1024]{1,0:T(8,128)(2,1)}, bf16[256,1024]{1,0:T(8,128)(2,1)}) custom-call(s32[16]{0:T(128)} %reshape.110.chosen_ref, s32[16]{0:T(128)} %reshape.116.filled_ref, f32[256,2048]{1,0:T(8,128)} %get-tuple-element.12.own_ref, bf16[64,2048]{1,0:T(8,128)(2,1)} %pad_maximum_fusion.1.edge_ref, bf16[16,32,2048]{2,1,0:T(8,128)(2,1)} %bitcast.3.inbound_ref), custom_call_target="tpu_custom_call" | custom-call | tf_op jit(solution)/shard_map/pallas_call | solution.py:370
  130.9 1.3 copy.16
  (8 shorter events, 0.1 us)
Async XLA Ops:
  4.7 1.0 copy-start.2
  8.4 9.1 %copy-start.4 = (s32[256]{0:T(256)S(1)}, s32[256]{0:T(256)}, u32[]{:S(2)}) copy-start(s32[256]{0:T(256)} %param.12) | copy-start | bytes 3076
  8.4 30.1 %all-to-all-start = ((bf16[4,4,32,2048]{3,2,1,0:T(8,128)(2,1)}), bf16[4,4,32,2048]{3,2,1,0:T(8,128)(2,1)S(1)}, u32[]{:S(2)}, u32[]{:S(2)}) async-start(bf16[4,4,32,2048]{3,2,1,0:T(8,128)(2,1)} %bitcast.8), calls=%async_computation | async-start | bytes 4194304 | tf_op jit(solution)/shard_map/all_to_all | solution.py:331
  13.8 6.4 %collective-permute-start = (bf16[32,2048]{1,0:T(8,128)(2,1)S(1)}, bf16[32,2048]{1,0:T(8,128)(2,1)S(1)}, u32[]{:S(2)}, u32[]{:S(2)}) collective-permute-start(bf16[32,2048]{1,0:T(8,128)(2,1)S(1)} %get-tuple-element.23), channel_id=1, source_target_pairs={{0,1},{1,2},{2,3},{4,5},{5,6},{6,7},{8,9},{9,10},{10,11},{12,13},{... | collective-permute-start | bytes 393224 | tf_op jit(solution)/shard_map/ppermute | solution.py:285
  16.2 4.7 %collective-permute-start.1 = (bf16[32,2048]{1,0:T(8,128)(2,1)S(1)}, bf16[32,2048]{1,0:T(8,128)(2,1)S(1)}, u32[]{:S(2)}, u32[]{:S(2)}) collective-permute-start(bf16[32,2048]{1,0:T(8,128)(2,1)S(1)} %get-tuple-element.24), channel_id=1, source_target_pairs={{1,0},{2,1},{3,2},{5,4},{6,5},{7,6},{9,8},{10,9},{11,10},{13,12},{... | collective-permute-start | bytes 393224 | tf_op jit(solution)/shard_map/ppermute | solution.py:286
  38.5 1.3 copy-start.1
  65.5 4.6 %copy-start.3 = (bf16[64,2048]{1,0:T(8,128)(2,1)S(1)}, bf16[64,2048]{1,0:T(8,128)(2,1)}, u32[]{:S(2)}) copy-start(bf16[64,2048]{1,0:T(8,128)(2,1)} %get-tuple-element.13) | copy-start | bytes 786436
  65.5 61.4 %all-to-all-start.1 = ((bf16[4,4,32,2048]{3,2,1,0:T(8,128)(2,1)}), bf16[4,4,32,2048]{3,2,1,0:T(8,128)(2,1)}, u32[]{:S(2)}, u32[]{:S(2)}) async-start(bf16[4,4,32,2048]{3,2,1,0:T(8,128)(2,1)} %bitcast.10), calls=%async_computation.1 | async-start | bytes 4194304 | tf_op jit(solution)/shard_map/all_to_all | solution.py:331
  70.1 56.1 %collective-permute-start.2 = (bf16[32,2048]{1,0:T(8,128)(2,1)S(1)}, bf16[32,2048]{1,0:T(8,128)(2,1)S(1)}, u32[]{:S(2)}, u32[]{:S(2)}) collective-permute-start(bf16[32,2048]{1,0:T(8,128)(2,1)S(1)} %get-tuple-element.25), channel_id=1, source_target_pairs={{0,1},{1,2},{2,3},{4,5},{5,6},{6,7},{8,9},{9,10},{10,11},{12,13},{... | collective-permute-start | bytes 393224 | tf_op jit(solution)/shard_map/ppermute | solution.py:285
  74.0 52.2 %collective-permute-start.3 = (bf16[32,2048]{1,0:T(8,128)(2,1)S(1)}, bf16[32,2048]{1,0:T(8,128)(2,1)S(1)}, u32[]{:S(2)}, u32[]{:S(2)}) collective-permute-start(bf16[32,2048]{1,0:T(8,128)(2,1)S(1)} %get-tuple-element.26), channel_id=1, source_target_pairs={{1,0},{2,1},{3,2},{5,4},{6,5},{7,6},{9,8},{10,9},{11,10},{13,12},{... | collective-permute-start | bytes 393224 | tf_op jit(solution)/shard_map/ppermute | solution.py:286
  75.9 1.6 %copy-start = (bf16[1024,1024]{1,0:T(8,128)(2,1)S(1)}, bf16[1024,1024]{1,0:T(8,128)(2,1)}, u32[]{:S(2)}) copy-start(bf16[1024,1024]{1,0:T(8,128)(2,1)} %get-tuple-element.17) | copy-start | bytes 6291460

commit v3 on v2

--- a/solution.py
+++ b/solution.py
@@ -28,13 +28,13 @@
     slot_ref,
     live_ref,
     edge_ref,
+    near_ref,
+    source_ref,
     query_ref,
     grad_ref,
     mask_ref,
     weight_ref,
-    pair_ref,
-    edges_in_ref,
-    arrived_ref,
+    gathered_ref,
     query_grad_ref,
     own_ref,
     edge_out_ref,
@@ -57,9 +57,8 @@
         cols = pl.ds(pl.multiple_of(g * WIDE, WIDE), WIDE)
         attn[:, cols] = dot(hit[...], weight_ref[cols, :], NT).astype(jnp.bfloat16)
 
-    extended[:BLOCK, :] = edges_in_ref[:BLOCK, :]
-    extended[BLOCK : BLOCK + rows, :] = pair_ref[...]
-    extended[BLOCK + rows :, :] = edges_in_ref[BLOCK:, :]
+    for i in range(blocks + 2):
+        extended[i * BLOCK : (i + 1) * BLOCK, :] = gathered_ref[near_ref[i]]
     totals[...] = jnp.zeros_like(totals)
     outbound_ref[...] = jnp.zeros_like(outbound_ref)
 
@@ -81,20 +80,19 @@
         band = pl.ds(pl.multiple_of(n * BLOCK, BLOCK), 3 * BLOCK)
         allowed = jnp.where(key_block == 0, edge_ref[0, n], edge_ref[1, n] * (key_block == 2))
         allowed = jnp.where(key_block == 1, 1, allowed)
-        slots = []
+        slots = [slot_ref[n, f] for f in range(far_slots)]
+        sources = [source_ref[n, f] for f in range(far_slots)]
         for f in range(far_slots):
-            live = live_ref[n, f]
-            slots.append(jnp.where(live > 0, slot_ref[n, f], 0))
-            allowed = jnp.where(key_block == 3 + f, live, allowed)
+            allowed = jnp.where(key_block == 3 + f, live_ref[n, f], allowed)
         allowed = allowed > 0
         for g in range(groups):
             kc = pl.ds(g * WIDE, WIDE)
             vc = pl.ds(features + g * WIDE, WIDE)
             key = jnp.concatenate(
-                [extended[band, kc]] + [arrived_ref[s, :, kc] for s in slots], axis=0
+                [extended[band, kc]] + [gathered_ref[s, :, kc] for s in sources], axis=0
             )
             value = jnp.concatenate(
-                [extended[band, vc]] + [arrived_ref[s, :, vc] for s in slots], axis=0
+                [extended[band, vc]] + [gathered_ref[s, :, vc] for s in sources], axis=0
             )
             query = query_ref[at, kc] * jnp.bfloat16(HEAD_DIM**-0.5)
             query = jnp.concatenate([query] * GROUP, axis=0) * diagonal
@@ -131,10 +129,61 @@
         weight_out_ref[cols, :] = dot(attended[:, cols], hit[...], TN).astype(jnp.bfloat16)
 
 
-def gather_kernel(slot_total, chosen_ref, pair_ref, out_ref):
-    for s in range(slot_total):
-        at = pl.ds(pl.multiple_of(chosen_ref[s] * BLOCK, BLOCK), BLOCK)
-        out_ref[s] = pair_ref[at, :]
+def spread(index, count):
+    result, remaining = 0, index
+    for bit in bits_of(count):
+        result = result + (remaining % 2) * (count // (2 * bit))
+        remaining = remaining // 2
+    return result
+
+
+def gather_kernel(count, key_ref, value_ref, out_ref, send_sem, recv_sem):
+    blocks = out_ref.shape[0]
+    features = key_ref.shape[1]
+    me, row = lax.axis_index("off"), lax.axis_index("mid")
+    order = bits_of(count)[::-1]
+
+    def bit_of(bit):
+        return (me // bit) % 2
+
+    def partner(bit):
+        return (row, me + bit - 2 * bit * bit_of(bit))
+
+    barrier = pltpu.get_barrier_semaphore()
+    for bit in order:
+        pl.semaphore_signal(
+            barrier, inc=1, device_id=partner(bit), device_id_type=pl.DeviceIdType.MESH
+        )
+    place = spread(me, count)
+    for b in range(blocks):
+        at = slice(b * BLOCK, (b + 1) * BLOCK)
+        out_ref[b, place, :, :features] = key_ref[at, :]
+        out_ref[b, place, :, features:] = value_ref[at, :]
+    pl.semaphore_wait(barrier, len(order))
+
+    def send(b, i):
+        bit = order[i]
+        held = out_ref.at[b, pl.ds(place // (1 << i) * (1 << i), 1 << i)]
+        return pltpu.make_async_remote_copy(
+            src_ref=held,
+            dst_ref=held,
+            send_sem=send_sem.at[b, i],
+            recv_sem=recv_sem.at[b, i],
+            device_id=partner(bit),
+            device_id_type=pl.DeviceIdType.MESH,
+        )
+
+    copies = []
+    for b in range(blocks):
+        copies.append(send(b, 0))
+        copies[b].start()
+    for i in range(1, len(order)):
+        for b in range(blocks):
+            copies[b].wait()
+            copies[b] = send(b, i)
+            copies[b].start()
+    for copy in copies:
+        copy.wait()
 
 
 def finish_kernel(
@@ -167,15 +216,19 @@
 def chain_orders(mid_size, off_size):
     off_bits = [("off", b) for b in bits_of(off_size)]
     mid_bits = [("mid", b) for b in bits_of(mid_size)]
-    first = off_bits[:1] + mid_bits + off_bits[1:]
-    second = off_bits[:1] + mid_bits[1:2] + mid_bits[:1] + mid_bits[2:] + off_bits[1:]
-    return first, second
+    swapped = mid_bits[1:2] + mid_bits[:1] + mid_bits[2:]
+    turned = mid_bits[1:] + mid_bits[:1]
+    later = mid_bits[:1] + mid_bits[2:] + mid_bits[1:2]
+    return [off_bits[:1] + mids + off_bits[1:] for mids in (mid_bits, swapped, later, turned)]
 
 
 def weight_sum_kernel(orders, scale, part_ref, out_ref, held, landed, whole, send_sem, recv_sem):
-    pieces = part_ref.shape[0]
+    pieces, _, wide = held.shape
     steps = len(orders[0])
-    span = pieces // 2
+    chains = len(orders)
+    span = pieces // chains
+    splits = part_ref.shape[1] // wide
+    tall = pieces // splits
     place = {"mid": lax.axis_index("mid"), "off": lax.axis_index("off")}
 
     def bit_of(axis, bit):
@@ -190,7 +243,9 @@
         pl.semaphore_signal(
             barrier, inc=1, device_id=partner(axis, bit), device_id_type=pl.DeviceIdType.MESH
         )
-    held[...] = part_ref[...]
+    for j in range(splits):
+        cols = slice(j * wide, (j + 1) * wide)
+        held[j * tall : (j + 1) * tall] = part_ref[:, cols].reshape(tall, 16, wide)
     pl.semaphore_wait(barrier, steps)
 
     starts = [[None] * (steps + 1) for _ in orders]
@@ -224,12 +279,12 @@
         mine = whole.at[pl.ds(starts[c][i + 1], size)]
         return remote(mine, mine, c, steps + i, axis, bit)
 
-    copies = [halve(c, 0) for c in range(2)]
+    copies = [halve(c, 0) for c in range(chains)]
     for copy in copies:
         copy.start()
     for i in range(steps):
         size = span >> (i + 1)
-        for c in range(2):
+        for c in range(chains):
             copies[c].wait()
             at = pl.ds(starts[c][i + 1], size)
             room = c * span + span - 2 * size
@@ -242,32 +297,33 @@
                 copies[c] = double(c, i)
             copies[c].start()
     for i in reversed(range(steps)):
-        for c in range(2):
+        for c in range(chains):
             copies[c].wait()
             if i > 0:
                 copies[c] = double(c, i - 1)
                 copies[c].start()
-    out_ref[...] = whole[...]
+    for j in range(splits):
+        cols = slice(j * wide, (j + 1) * wide)
+        out_ref[:, cols] = whole[j * tall : (j + 1) * tall].reshape(tall * 16, wide)
 
 
 def weight_sum(part, mid_size, off_size, scale):
     rows, columns = part.shape
     orders = chain_orders(mid_size, off_size)
     steps = len(orders[0])
-    splits = max(1, 32 * mid_size * off_size // rows)
+    splits = max(1, 16 * len(orders) * mid_size * off_size // rows)
     pieces, wide = splits * rows // 16, columns // splits
-    part = part.reshape(rows // 16, 16, splits, wide).transpose(2, 0, 1, 3)
-    total = pl.pallas_call(
+    return pl.pallas_call(
         functools.partial(weight_sum_kernel, orders, scale),
-        out_shape=jax.ShapeDtypeStruct((pieces, 16, wide), jnp.bfloat16),
+        out_shape=jax.ShapeDtypeStruct((rows, columns), jnp.bfloat16),
         in_specs=[VMEM],
         out_specs=VMEM,
         scratch_shapes=[
             pltpu.VMEM((pieces, 16, wide), jnp.bfloat16),
             pltpu.VMEM((pieces, 16, wide), jnp.bfloat16),
             pltpu.VMEM((pieces, 16, wide), jnp.bfloat16),
-            pltpu.SemaphoreType.DMA((2, 2 * steps)),
-            pltpu.SemaphoreType.DMA((2, 2 * steps)),
+            pltpu.SemaphoreType.DMA((len(orders), 2 * steps)),
+            pltpu.SemaphoreType.DMA((len(orders), 2 * steps)),
         ],
         compiler_params=pltpu.CompilerParams(
             vmem_limit_bytes=16 * 1024 * 1024, collective_id=0, has_side_effects=True
@@ -275,9 +331,7 @@
         cost_estimate=pl.CostEstimate(
             flops=2 * rows * columns, bytes_accessed=64 * rows * columns, transcendentals=0
         ),
-    )(part.reshape(pieces, 16, wide))
-    total = total.reshape(splits, rows // 16, 16, wide).transpose(1, 2, 0, 3)
-    return total.reshape(rows, columns)
+    )(part)
 
 
 def edge_swap(head, tail):
@@ -316,22 +370,32 @@
     global_block = position * blocks + jnp.arange(blocks)
     edge_ok = jnp.stack([global_block >= 1, global_block <= total_blocks - 2]).astype(jnp.int32)
 
-    pair_rows = jnp.concatenate([key_rows, value_rows], axis=1)
-    before, after = edge_swap(pair_rows[:BLOCK], pair_rows[row_count - BLOCK :])
-    outgoing = pl.pallas_call(
-        functools.partial(gather_kernel, slot_total),
-        out_shape=jax.ShapeDtypeStruct((slot_total, BLOCK, width), jnp.bfloat16),
-        in_specs=[SMEM, VMEM],
+    def stored_at(block):
+        return (block % blocks) * off_size + spread(block // blocks, off_size)
+
+    near = position * blocks - 1 + jnp.arange(blocks + 2)
+    near = stored_at(jnp.clip(near, 0, total_blocks - 1)).astype(jnp.int32)
+    mine_far = lax.dynamic_index_in_dim(far_table, position, 0, keepdims=False)
+    source = stored_at(jnp.maximum(mine_far, 0)).astype(jnp.int32)
+    gathered = pl.pallas_call(
+        functools.partial(gather_kernel, off_size),
+        out_shape=jax.ShapeDtypeStruct((blocks, off_size, BLOCK, width), jnp.bfloat16),
+        in_specs=[VMEM, VMEM],
         out_specs=VMEM,
-        compiler_params=pltpu.CompilerParams(vmem_limit_bytes=VMEM_LIMIT),
-    )(chosen, pair_rows)
+        scratch_shapes=[
+            pltpu.SemaphoreType.DMA((blocks, len(bits_of(off_size)))),
+            pltpu.SemaphoreType.DMA((blocks, len(bits_of(off_size)))),
+        ],
+        compiler_params=pltpu.CompilerParams(
+            vmem_limit_bytes=32 * 1024 * 1024, collective_id=1, has_side_effects=True
+        ),
+    )(key_rows, value_rows)
 
     def exchange(parts):
         parts = parts.reshape(off_size, capacity, BLOCK, width)
         parts = lax.all_to_all(parts, "off", split_axis=0, concat_axis=0, tiled=True)
         return parts.reshape(slot_total, BLOCK, width)
 
-    arrived = exchange(outgoing)
     query_grad, own, edges, outbound, weight_part = pl.pallas_call(
         functools.partial(attend_kernel, blocks, far_slots, slot_total),
         out_shape=(
@@ -341,7 +405,7 @@
             jax.ShapeDtypeStruct((slot_total, BLOCK, width), jnp.bfloat16),
             jax.ShapeDtypeStruct((features, features), jnp.bfloat16),
         ),
-        in_specs=[SMEM] * 3 + [VMEM] * 7,
+        in_specs=[SMEM] * 5 + [VMEM] * 5,
         out_specs=(VMEM,) * 5,
         scratch_shapes=[
             pltpu.VMEM((row_count, features), jnp.bfloat16),
@@ -355,13 +419,13 @@
         mine_slot.reshape(blocks, far_slots).astype(jnp.int32),
         mine_live.reshape(blocks, far_slots).astype(jnp.int32),
         edge_ok,
+        near,
+        source.reshape(blocks, far_slots),
         query_rows,
         grad_out,
         masked_rows[:, None].astype(jnp.bfloat16),
         out_weight,
-        pair_rows,
-        jnp.concatenate([before, after], axis=0),
-        arrived,
+        gathered.reshape(total_blocks, BLOCK, width),
     )
     inbound = exchange(outbound)
     before, after = edge_swap(edges[:BLOCK], edges[BLOCK:])

time: 133 us -> 129 us (0.970)
  Pallas kernels: 81 us -> 105 us
  waiting for transfers between devices: 17.6 us -> 0.01 us
  starting transfers between devices: 17.8 us -> 8.22 us
    pallas_call x1, Pallas kernels: 2.69 us -> 28.2 us  [on_device(): pl.pallas_call(functools.partial(gather_kernel, off_size), out_shape=jax....]
    all_to_all x2 -> x1, waiting for transfers between devices: 16.9 us -> 0.01 us  [exchange(): lax.all_to_all(parts, 'off', split_axis=0, concat_axis=0, tiled=True)]
    all_to_all x2 -> x1, starting transfers between devices: 8.95 us -> 4.57 us  [exchange(): lax.all_to_all(parts, 'off', split_axis=0, concat_axis=0, tiled=True)]
    ppermute x2 -> x1, starting transfers between devices: 6.25 us -> 2.36 us  [edge_swap(): before = lax.ppermute(tail, 'off', [(i, i + 1) for i in range(count - 1)])]
    pallas_call x1, Pallas kernels: 48.6 us -> 47 us  [weight_sum(): pl.pallas_call(functools.partial(weight_sum_kernel, orders, scale), out_s...]
    unnamed x13 -> x12, local copies, waits for them, and re-layouts: 7.07 us -> 7.67 us
  transfers between devices with their start and end apart: 6 -> 3, of which waited for: 2 -> 0; matrix products, arithmetic and copies ran while one was open for 4% -> 2% of each run, Pallas kernels for 37% -> 36%
where the time goes in v3:
time: 129 us
  Pallas kernels  105 us (81%)
  local copies, waits for them, and re-layouts  11.3 us (9%)
  starting transfers between devices  8.22 us (6%)
  other arithmetic  3.71 us (3%)
    pallas_call x1, Pallas kernels, weight_sum(): pl.pallas_call(functools.partial(weight_sum_kernel, orders, scale), out_s...  47 us
    pallas_call x1, Pallas kernels, on_device(): pl.pallas_call(functools.partial(gather_kernel, off_size), out_shape=jax....  28.2 us
    pallas_call x1, Pallas kernels, on_device(): pl.pallas_call(functools.partial(attend_kernel, blocks, far_slots, slot_t...  25.9 us
    unnamed x12, local copies, waits for them, and re-layouts  7.67 us
    all_to_all x1, starting transfers between devices, exchange(): lax.all_to_all(parts, 'off', split_axis=0, concat_axis=0, tiled=True)  4.57 us
    pallas_call x1, Pallas kernels, on_device(): pl.pallas_call(functools.partial(finish_kernel, slot_total), out_shape=(j...  3.96 us
  transfers between devices with their start and end apart: 3, of which 0 were waited for; matrix products, arithmetic and copies ran while one was open for 2% of the time, Pallas kernels for 36%

profile of v3, /device:TPU:0, one launch (start us, length us, event | category | flops | bytes accessed | tf_op | source)
XLA Modules:
  0.0 129.1 jit_solution(16653137052510965058)
XLA Ops:
  0.7 0.5 fusion.14.near_ref
  1.2 0.7 convert_element_type.25
  1.8 0.8 copy.12
  2.6 0.1 reshape.117
  2.7 0.1 ne.121
  2.8 0.1 fusion
  2.9 0.2 select_reduce_fusion.1
  3.2 0.7 reshape.122.live_ref
  3.9 0.7 select_n.97.slot_ref
  4.5 0.1 rem.155
  4.6 0.1 div.63
  4.7 0.7 convert_element_type.31.mask_ref
  5.4 0.5 add_convert_fusion.edge_ref
  6.0 0.0 copy-start.2
  6.0 1.0 copy-done.2
  7.0 0.0 copy-start.3
  7.0 1.0 copy-done.3
  8.1 28.2 %shard_map.102 = bf16[8,4,32,2048]{3,2,1,0:T(8,128)(2,1)S(1)} custom-call(bf16[256,1024]{1,0:T(8,128)(2,1)S(1)} %copy-done.2, bf16[256,1024]{1,0:T(8,128)(2,1)S(1)} %copy-done.3), custom_call_target="tpu_custom_call" | custom-call | tf_op jit(solution)/shard_map/pallas_call | solution.py:380
  36.3 0.0 copy-start
  36.3 1.9 %copy-done = bf16[8,4,32,2048]{3,2,1,0:T(8,128)(2,1)} copy-done((bf16[8,4,32,2048]{3,2,1,0:T(8,128)(2,1)}, bf16[8,4,32,2048]{3,2,1,0:T(8,128)(2,1)S(1)}, u32[]{:S(2)}) %copy-start) | copy-done | bytes 4194328
  38.2 0.6 fusion.4.source_ref
  38.8 25.9 %shard_map.103 = (bf16[256,1024]{1,0:T(8,128)(2,1)}, f32[256,2048]{1,0:T(8,128)}, bf16[64,2048]{1,0:T(8,128)(2,1)}, bf16[16,32,2048]{2,1,0:T(8,128)(2,1)}, bf16[1024,1024]{1,0:T(8,128)(2,1)}) custom-call(s32[8,2]{1,0:T(8,128)} %select_n.97.slot_ref, s32[8,2]{1,0:T(8,128)} %reshape.122.live_ref, s32[2,8]{1,0:T(2,128)} %add_convert_fusion.edge_ref, ...), custom_call_target="tpu_custom_call" | custom-call | tf_op jit(solution)/shard_map/pallas_call | solution.py:399
  64.7 0.0 copy-start.4
  64.7 4.6 %all-to-all-start = ((bf16[4,4,32,2048]{3,2,1,0:T(8,128)(2,1)}), bf16[4,4,32,2048]{3,2,1,0:T(8,128)(2,1)}, u32[]{:S(2)}, u32[]{:S(2)}) async-start(bf16[4,4,32,2048]{3,2,1,0:T(8,128)(2,1)} %bitcast.4), calls=%async_computation | async-start | bytes 4194304 | tf_op jit(solution)/shard_map/all_to_all | solution.py:396
  69.3 0.0 copy-done.4
  69.3 2.4 %collective-permute-start = (bf16[32,2048]{1,0:T(8,128)(2,1)S(1)}, bf16[32,2048]{1,0:T(8,128)(2,1)S(1)}, u32[]{:S(2)}, u32[]{:S(2)}) collective-permute-start(bf16[32,2048]{1,0:T(8,128)(2,1)S(1)} %get-tuple-element.25), channel_id=1, source_target_pairs={{0,1},{1,2},{2,3},{4,5},{5,6},{6,7},{8,9},{9,10},{10,11},{12,13},{... | collective-permute-start | bytes 393224 | tf_op jit(solution)/shard_map/ppermute | solution.py:339
  71.7 1.3 %collective-permute-start.1 = (bf16[32,2048]{1,0:T(8,128)(2,1)S(1)}, bf16[32,2048]{1,0:T(8,128)(2,1)S(1)}, u32[]{:S(2)}, u32[]{:S(2)}) collective-permute-start(bf16[32,2048]{1,0:T(8,128)(2,1)S(1)} %get-tuple-element.26), channel_id=1, source_target_pairs={{1,0},{2,1},{3,2},{5,4},{6,5},{7,6},{9,8},{10,9},{11,10},{13,12},{... | collective-permute-start | bytes 393224 | tf_op jit(solution)/shard_map/ppermute | solution.py:340
  73.0 0.1 select_reduce_fusion
  73.1 0.6 reshape.119.chosen_ref
  73.7 0.1 fusion.2
  73.8 0.6 reshape.123.filled_ref
  74.4 0.0 copy-start.1
  74.4 1.6 %copy-done.1 = bf16[1024,1024]{1,0:T(8,128)(2,1)S(1)} copy-done((bf16[1024,1024]{1,0:T(8,128)(2,1)S(1)}, bf16[1024,1024]{1,0:T(8,128)(2,1)}, u32[]{:S(2)}) %copy-start.1) | copy-done | bytes 2097176
  76.0 47.0 %shard_map.105 = bf16[1024,1024]{1,0:T(8,128)(2,1)S(1)} custom-call(bf16[1024,1024]{1,0:T(8,128)(2,1)S(1)} %copy-done.1), custom_call_target="tpu_custom_call" | custom-call | flops 2097152 | bytes 67108864 | tf_op jit(solution)/shard_map/pallas_call | solution.py:316
  123.0 0.0 collective-permute-done
  123.0 0.0 collective-permute-done.1
  123.0 0.7 pad_maximum_fusion.edge_ref
  123.8 0.0 all-to-all-done
  123.8 4.0 %shard_map.104 = (bf16[256,1024]{1,0:T(8,128)(2,1)}, bf16[256,1024]{1,0:T(8,128)(2,1)}) custom-call(s32[16]{0:T(128)} %reshape.119.chosen_ref, s32[16]{0:T(128)} %reshape.123.filled_ref, f32[256,2048]{1,0:T(8,128)} %get-tuple-element.12.own_ref, bf16[64,2048]{1,0:T(8,128)(2,1)} %pad_maximum_fusion.edge_ref, bf16[16,32,2048]{2,1,0:T(8,128)(2,1)} %bitcast.2.inbound_ref), custom_call_target="tpu_custom_call" | custom-call | tf_op jit(solution)/shard_map/pallas_call | solution.py:434
  127.7 1.3 %copy.15 = bf16[1024,1024]{1,0:T(8,128)(2,1)} copy(bf16[1024,1024]{1,0:T(8,128)(2,1)S(1)} %shard_map.105) | data formatting | bytes 4194304
  (8 shorter events, 0.2 us)
Async XLA Ops:
  6.0 1.0 copy-start.2
  7.0 1.0 copy-start.3
  36.3 1.9 %copy-start = (bf16[8,4,32,2048]{3,2,1,0:T(8,128)(2,1)}, bf16[8,4,32,2048]{3,2,1,0:T(8,128)(2,1)S(1)}, u32[]{:S(2)}) copy-start(bf16[8,4,32,2048]{3,2,1,0:T(8,128)(2,1)S(1)} %shard_map.102) | copy-start | bytes 12582916
  64.7 4.6 %copy-start.4 = (bf16[64,2048]{1,0:T(8,128)(2,1)S(1)}, bf16[64,2048]{1,0:T(8,128)(2,1)}, u32[]{:S(2)}) copy-start(bf16[64,2048]{1,0:T(8,128)(2,1)} %get-tuple-element.13) | copy-start | bytes 786436
  64.7 59.1 %all-to-all-start = ((bf16[4,4,32,2048]{3,2,1,0:T(8,128)(2,1)}), bf16[4,4,32,2048]{3,2,1,0:T(8,128)(2,1)}, u32[]{:S(2)}, u32[]{:S(2)}) async-start(bf16[4,4,32,2048]{3,2,1,0:T(8,128)(2,1)} %bitcast.4), calls=%async_computation | async-start | bytes 4194304 | tf_op jit(solution)/shard_map/all_to_all | solution.py:396
  69.3 53.7 %collective-permute-start = (bf16[32,2048]{1,0:T(8,128)(2,1)S(1)}, bf16[32,2048]{1,0:T(8,128)(2,1)S(1)}, u32[]{:S(2)}, u32[]{:S(2)}) collective-permute-start(bf16[32,2048]{1,0:T(8,128)(2,1)S(1)} %get-tuple-element.25), channel_id=1, source_target_pairs={{0,1},{1,2},{2,3},{4,5},{5,6},{6,7},{8,9},{9,10},{10,11},{12,13},{... | collective-permute-start | bytes 393224 | tf_op jit(solution)/shard_map/ppermute | solution.py:339
  71.7 51.3 %collective-permute-start.1 = (bf16[32,2048]{1,0:T(8,128)(2,1)S(1)}, bf16[32,2048]{1,0:T(8,128)(2,1)S(1)}, u32[]{:S(2)}, u32[]{:S(2)}) collective-permute-start(bf16[32,2048]{1,0:T(8,128)(2,1)S(1)} %get-tuple-element.26), channel_id=1, source_target_pairs={{1,0},{2,1},{3,2},{5,4},{6,5},{7,6},{9,8},{10,9},{11,10},{13,12},{... | collective-permute-start | bytes 393224 | tf_op jit(solution)/shard_map/ppermute | solution.py:340
  74.4 1.6 %copy-start.1 = (bf16[1024,1024]{1,0:T(8,128)(2,1)S(1)}, bf16[1024,1024]{1,0:T(8,128)(2,1)}, u32[]{:S(2)}) copy-start(bf16[1024,1024]{1,0:T(8,128)(2,1)} %get-tuple-element.17.part_ref) | copy-start | bytes 6291460

commit v4 on v3

--- a/solution.py
+++ b/solution.py
@@ -31,17 +31,14 @@
     near_ref,
     source_ref,
     query_ref,
-    grad_ref,
-    mask_ref,
-    weight_ref,
+    hit,
+    attn,
     gathered_ref,
     query_grad_ref,
     own_ref,
     edge_out_ref,
     outbound_ref,
     weight_out_ref,
-    hit,
-    attn,
     attended,
     extended,
     totals,
@@ -50,13 +47,6 @@
     groups = features // WIDE
     stack = GROUP * BLOCK
     keys = (3 + far_slots) * BLOCK
-    hit[...] = grad_ref[...] * mask_ref[...]
-
-    @pl.loop(0, groups)
-    def _(g):
-        cols = pl.ds(pl.multiple_of(g * WIDE, WIDE), WIDE)
-        attn[:, cols] = dot(hit[...], weight_ref[cols, :], NT).astype(jnp.bfloat16)
-
     for i in range(blocks + 2):
         extended[i * BLOCK : (i + 1) * BLOCK, :] = gathered_ref[near_ref[i]]
     totals[...] = jnp.zeros_like(totals)
@@ -137,7 +127,19 @@
     return result
 
 
-def gather_kernel(count, key_ref, value_ref, out_ref, send_sem, recv_sem):
+def gather_kernel(
+    count,
+    key_ref,
+    value_ref,
+    grad_ref,
+    mask_ref,
+    weight_ref,
+    out_ref,
+    hit_ref,
+    attn_ref,
+    send_sem,
+    recv_sem,
+):
     blocks = out_ref.shape[0]
     features = key_ref.shape[1]
     me, row = lax.axis_index("off"), lax.axis_index("mid")
@@ -177,6 +179,10 @@
     for b in range(blocks):
         copies.append(send(b, 0))
         copies[b].start()
+    hit_ref[...] = grad_ref[...] * mask_ref[...]
+    for g in range(features // WIDE):
+        cols = slice(g * WIDE, (g + 1) * WIDE)
+        attn_ref[:, cols] = dot(hit_ref[...], weight_ref[cols, :], NT).astype(jnp.bfloat16)
     for i in range(1, len(order)):
         for b in range(blocks):
             copies[b].wait()
@@ -377,11 +383,15 @@
     near = stored_at(jnp.clip(near, 0, total_blocks - 1)).astype(jnp.int32)
     mine_far = lax.dynamic_index_in_dim(far_table, position, 0, keepdims=False)
     source = stored_at(jnp.maximum(mine_far, 0)).astype(jnp.int32)
-    gathered = pl.pallas_call(
+    gathered, hit, attn = pl.pallas_call(
         functools.partial(gather_kernel, off_size),
-        out_shape=jax.ShapeDtypeStruct((blocks, off_size, BLOCK, width), jnp.bfloat16),
-        in_specs=[VMEM, VMEM],
-        out_specs=VMEM,
+        out_shape=(
+            jax.ShapeDtypeStruct((blocks, off_size, BLOCK, width), jnp.bfloat16),
+            jax.ShapeDtypeStruct((row_count, features), jnp.bfloat16),
+            jax.ShapeDtypeStruct((row_count, features), jnp.bfloat16),
+        ),
+        in_specs=[VMEM] * 5,
+        out_specs=(VMEM,) * 3,
         scratch_shapes=[
             pltpu.SemaphoreType.DMA((blocks, len(bits_of(off_size)))),
             pltpu.SemaphoreType.DMA((blocks, len(bits_of(off_size)))),
@@ -389,7 +399,13 @@
         compiler_params=pltpu.CompilerParams(
             vmem_limit_bytes=32 * 1024 * 1024, collective_id=1, has_side_effects=True
         ),
-    )(key_rows, value_rows)
+    )(
+        key_rows,
+        value_rows,
+        grad_out,
+        masked_rows[:, None].astype(jnp.bfloat16),
+        out_weight,
+    )
 
     def exchange(parts):
         parts = parts.reshape(off_size, capacity, BLOCK, width)
@@ -405,11 +421,9 @@
             jax.ShapeDtypeStruct((slot_total, BLOCK, width), jnp.bfloat16),
             jax.ShapeDtypeStruct((features, features), jnp.bfloat16),
         ),
-        in_specs=[SMEM] * 5 + [VMEM] * 5,
+        in_specs=[SMEM] * 5 + [VMEM] * 4,
         out_specs=(VMEM,) * 5,
         scratch_shapes=[
-            pltpu.VMEM((row_count, features), jnp.bfloat16),
-            pltpu.VMEM((row_count, features), jnp.bfloat16),
             pltpu.VMEM((row_count, features), jnp.bfloat16),
             pltpu.VMEM((row_count + 2 * BLOCK, width), jnp.bfloat16),
             pltpu.VMEM((row_count + 2 * BLOCK, width), jnp.float32),
@@ -422,9 +436,8 @@
         near,
         source.reshape(blocks, far_slots),
         query_rows,
-        grad_out,
-        masked_rows[:, None].astype(jnp.bfloat16),
-        out_weight,
+        hit,
+        attn,
         gathered.reshape(total_blocks, BLOCK, width),
     )
     inbound = exchange(outbound)

time: 129 us -> 131 us (1.016)
  local copies, waits for them, and re-layouts: 11.3 us -> 14.9 us
  Pallas kernels: 105 us -> 103 us
    unnamed x12 -> x20, local copies, waits for them, and re-layouts: 7.67 us -> 11.9 us
    pallas_call x1, Pallas kernels: 25.9 us -> 24 us  [on_device(): pl.pallas_call(functools.partial(attend_kernel, blocks, far_slots, slot_t...]
where the time goes in v4:
time: 131 us
  Pallas kernels  103 us (79%)
  local copies, waits for them, and re-layouts  14.9 us (11%)
  starting transfers between devices  8.22 us (6%)
  other arithmetic  3.77 us (3%)
    pallas_call x1, Pallas kernels, weight_sum(): pl.pallas_call(functools.partial(weight_sum_kernel, orders, scale), out_s...  47 us
    pallas_call x1, Pallas kernels, on_device(): pl.pallas_call(functools.partial(gather_kernel, off_size), out_shape=(jax...  28.2 us
    pallas_call x1, Pallas kernels, on_device(): pl.pallas_call(functools.partial(attend_kernel, blocks, far_slots, slot_t...  24 us
    unnamed x20, local copies, waits for them, and re-layouts  11.9 us
    all_to_all x1, starting transfers between devices, exchange(): lax.all_to_all(parts, 'off', split_axis=0, concat_axis=0, tiled=True)  4.57 us
    pallas_call x1, Pallas kernels, on_device(): pl.pallas_call(functools.partial(finish_kernel, slot_total), out_shape=(j...  3.96 us
  transfers between devices with their start and end apart: 3, of which 0 were waited for; matrix products, arithmetic and copies ran while one was open for 2% of the time, Pallas kernels for 36%

profile of v4, /device:TPU:0, one launch (start us, length us, event | category | flops | bytes accessed | tf_op | source)
XLA Modules:
  0.0 130.9 jit_solution(14735728497970936410)
XLA Ops:
  0.7 0.6 fusion.14.near_ref
  1.2 0.7 convert_element_type.25
  1.9 0.8 copy.12
  2.7 0.1 reshape.117
  2.8 0.1 ne.121
  2.9 0.1 fusion
  3.0 0.2 select_reduce_fusion.1
  3.3 0.7 reshape.122.live_ref
  3.9 0.7 select_n.97.slot_ref
  4.6 0.1 rem.155
  4.7 0.1 div.63
  4.8 0.1 convert_element_type.31.mask_ref
  4.9 0.5 add_convert_fusion.edge_ref
  5.4 0.6 fusion.4.source_ref
  6.0 0.0 copy-start.1
  6.0 1.6 %copy-done.1 = bf16[1024,1024]{1,0:T(8,128)(2,1)S(1)} copy-done((bf16[1024,1024]{1,0:T(8,128)(2,1)S(1)}, bf16[1024,1024]{1,0:T(8,128)(2,1)}, u32[]{:S(2)}) %copy-start.1) | copy-done | bytes 2097176
  7.6 0.0 copy-start.3
  7.6 1.0 copy-done.3
  8.7 0.0 copy-start.4
  8.7 1.0 copy-done.4
  9.7 0.0 copy-start.5
  9.7 1.0 copy-done.5
  10.7 28.2 %shard_map.102 = (bf16[8,4,32,2048]{3,2,1,0:T(8,128)(2,1)S(1)}, bf16[256,1024]{1,0:T(8,128)(2,1)S(1)}, bf16[256,1024]{1,0:T(8,128)(2,1)S(1)}) custom-call(bf16[256,1024]{1,0:T(8,128)(2,1)S(1)} %copy-done.3, bf16[256,1024]{1,0:T(8,128)(2,1)S(1)} %copy-done.4, bf16[256,1024]{1,0:T(8,128)(2,1)S(1)} %copy-done.5, ...), custom_call_target="tpu_custom_call" | custom-call | tf_op jit(solution)/shard_map/pallas_call | solution.py:386
  39.0 0.0 copy-start
  39.0 1.9 %copy-done = bf16[8,4,32,2048]{3,2,1,0:T(8,128)(2,1)} copy-done((bf16[8,4,32,2048]{3,2,1,0:T(8,128)(2,1)}, bf16[8,4,32,2048]{3,2,1,0:T(8,128)(2,1)S(1)}, u32[]{:S(2)}) %copy-start) | copy-done | bytes 4194328
  40.9 0.0 copy-start.6
  40.9 0.8 copy-done.6
  41.7 0.0 copy-start.7
  41.7 0.8 copy-done.7
  42.5 24.0 %shard_map.103 = (bf16[256,1024]{1,0:T(8,128)(2,1)}, f32[256,2048]{1,0:T(8,128)}, bf16[64,2048]{1,0:T(8,128)(2,1)}, bf16[16,32,2048]{2,1,0:T(8,128)(2,1)}, bf16[1024,1024]{1,0:T(8,128)(2,1)}) custom-call(s32[8,2]{1,0:T(8,128)} %select_n.97.slot_ref, s32[8,2]{1,0:T(8,128)} %reshape.122.live_ref, s32[2,8]{1,0:T(2,128)} %add_convert_fusion.edge_ref, ...), custom_call_target="tpu_custom_call" | custom-call | tf_op jit(solution)/shard_map/pallas_call | solution.py:415
  66.5 0.0 copy-start.8
  66.5 4.6 %all-to-all-start = ((bf16[4,4,32,2048]{3,2,1,0:T(8,128)(2,1)}), bf16[4,4,32,2048]{3,2,1,0:T(8,128)(2,1)}, u32[]{:S(2)}, u32[]{:S(2)}) async-start(bf16[4,4,32,2048]{3,2,1,0:T(8,128)(2,1)} %bitcast.4), calls=%async_computation | async-start | bytes 4194304 | tf_op jit(solution)/shard_map/all_to_all | solution.py:412
  71.1 0.0 copy-done.8
  71.1 2.4 %collective-permute-start = (bf16[32,2048]{1,0:T(8,128)(2,1)S(1)}, bf16[32,2048]{1,0:T(8,128)(2,1)S(1)}, u32[]{:S(2)}, u32[]{:S(2)}) collective-permute-start(bf16[32,2048]{1,0:T(8,128)(2,1)S(1)} %get-tuple-element.31), channel_id=1, source_target_pairs={{0,1},{1,2},{2,3},{4,5},{5,6},{6,7},{8,9},{9,10},{10,11},{12,13},{... | collective-permute-start | bytes 393224 | tf_op jit(solution)/shard_map/ppermute | solution.py:345
  73.5 1.3 collective-permute-start.1
  74.8 0.1 select_reduce_fusion
  74.9 0.6 reshape.119.chosen_ref
  75.5 0.1 fusion.2
  75.6 0.6 reshape.123.filled_ref
  76.2 0.0 copy-start.2
  76.2 1.6 %copy-done.2 = bf16[1024,1024]{1,0:T(8,128)(2,1)S(1)} copy-done((bf16[1024,1024]{1,0:T(8,128)(2,1)S(1)}, bf16[1024,1024]{1,0:T(8,128)(2,1)}, u32[]{:S(2)}) %copy-start.2) | copy-done | bytes 2097176
  77.8 47.0 %shard_map.105 = bf16[1024,1024]{1,0:T(8,128)(2,1)S(1)} custom-call(bf16[1024,1024]{1,0:T(8,128)(2,1)S(1)} %copy-done.2), custom_call_target="tpu_custom_call" | custom-call | flops 2097152 | bytes 67108864 | tf_op jit(solution)/shard_map/pallas_call | solution.py:322
  124.8 0.0 collective-permute-done
  124.9 0.0 collective-permute-done.1
  124.9 0.7 pad_maximum_fusion.edge_ref
  125.6 0.0 all-to-all-done
  125.6 4.0 %shard_map.104 = (bf16[256,1024]{1,0:T(8,128)(2,1)}, bf16[256,1024]{1,0:T(8,128)(2,1)}) custom-call(s32[16]{0:T(128)} %reshape.119.chosen_ref, s32[16]{0:T(128)} %reshape.123.filled_ref, f32[256,2048]{1,0:T(8,128)} %get-tuple-element.18.own_ref, bf16[64,2048]{1,0:T(8,128)(2,1)} %pad_maximum_fusion.edge_ref, bf16[16,32,2048]{2,1,0:T(8,128)(2,1)} %bitcast.2.inbound_ref), custom_call_target="tpu_custom_call" | custom-call | tf_op jit(solution)/shard_map/pallas_call | solution.py:447
  129.6 1.3 %copy.15 = bf16[1024,1024]{1,0:T(8,128)(2,1)} copy(bf16[1024,1024]{1,0:T(8,128)(2,1)S(1)} %shard_map.105) | data formatting | bytes 4194304
  (8 shorter events, 0.2 us)
Async XLA Ops:
  6.0 1.6 %copy-start.1 = (bf16[1024,1024]{1,0:T(8,128)(2,1)S(1)}, bf16[1024,1024]{1,0:T(8,128)(2,1)}, u32[]{:S(2)}) copy-start(bf16[1024,1024]{1,0:T(8,128)(2,1)} %weight_ref.1) | copy-start | bytes 6291460
  7.6 1.0 copy-start.3
  8.7 1.0 copy-start.4
  9.7 1.0 copy-start.5
  39.0 1.9 %copy-start = (bf16[8,4,32,2048]{3,2,1,0:T(8,128)(2,1)}, bf16[8,4,32,2048]{3,2,1,0:T(8,128)(2,1)S(1)}, u32[]{:S(2)}) copy-start(bf16[8,4,32,2048]{3,2,1,0:T(8,128)(2,1)S(1)} %get-tuple-element.16) | copy-start | bytes 12582916
  40.9 0.8 copy-start.6
  41.7 0.8 copy-start.7
  66.5 4.6 %copy-start.8 = (bf16[64,2048]{1,0:T(8,128)(2,1)S(1)}, bf16[64,2048]{1,0:T(8,128)(2,1)}, u32[]{:S(2)}) copy-start(bf16[64,2048]{1,0:T(8,128)(2,1)} %get-tuple-element.19) | copy-start | bytes 786436
  66.5 59.1 %all-to-all-start = ((bf16[4,4,32,2048]{3,2,1,0:T(8,128)(2,1)}), bf16[4,4,32,2048]{3,2,1,0:T(8,128)(2,1)}, u32[]{:S(2)}, u32[]{:S(2)}) async-start(bf16[4,4,32,2048]{3,2,1,0:T(8,128)(2,1)} %bitcast.4), calls=%async_computation | async-start | bytes 4194304 | tf_op jit(solution)/shard_map/all_to_all | solution.py:412
  71.1 53.7 %collective-permute-start = (bf16[32,2048]{1,0:T(8,128)(2,1)S(1)}, bf16[32,2048]{1,0:T(8,128)(2,1)S(1)}, u32[]{:S(2)}, u32[]{:S(2)}) collective-permute-start(bf16[32,2048]{1,0:T(8,128)(2,1)S(1)} %get-tuple-element.31), channel_id=1, source_target_pairs={{0,1},{1,2},{2,3},{4,5},{5,6},{6,7},{8,9},{9,10},{10,11},{12,13},{... | collective-permute-start | bytes 393224 | tf_op jit(solution)/shard_map/ppermute | solution.py:345
  73.5 51.3 %collective-permute-start.1 = (bf16[32,2048]{1,0:T(8,128)(2,1)S(1)}, bf16[32,2048]{1,0:T(8,128)(2,1)S(1)}, u32[]{:S(2)}, u32[]{:S(2)}) collective-permute-start(bf16[32,2048]{1,0:T(8,128)(2,1)S(1)} %get-tuple-element.32), channel_id=1, source_target_pairs={{1,0},{2,1},{3,2},{5,4},{6,5},{7,6},{9,8},{10,9},{11,10},{13,12},{... | collective-permute-start | bytes 393224 | tf_op jit(solution)/shard_map/ppermute | solution.py:346
  76.2 1.6 %copy-start.2 = (bf16[1024,1024]{1,0:T(8,128)(2,1)S(1)}, bf16[1024,1024]{1,0:T(8,128)(2,1)}, u32[]{:S(2)}) copy-start(bf16[1024,1024]{1,0:T(8,128)(2,1)} %get-tuple-element.23.part_ref) | copy-start | bytes 6291460

commit v5 on v3

--- a/solution.py
+++ b/solution.py
@@ -222,7 +222,23 @@
     return [off_bits[:1] + mids + off_bits[1:] for mids in (mid_bits, swapped, later, turned)]
 
 
-def weight_sum_kernel(orders, scale, part_ref, out_ref, held, landed, whole, send_sem, recv_sem):
+def weight_sum_kernel(
+    orders,
+    scale,
+    count,
+    part_ref,
+    edge_ref,
+    out_ref,
+    edge_out_ref,
+    held,
+    landed,
+    whole,
+    edge_landed,
+    send_sem,
+    recv_sem,
+    edge_send,
+    edge_recv,
+):
     pieces, _, wide = held.shape
     steps = len(orders[0])
     chains = len(orders)
@@ -243,10 +259,27 @@
         pl.semaphore_signal(
             barrier, inc=1, device_id=partner(axis, bit), device_id_type=pl.DeviceIdType.MESH
         )
+    sides = [(place["off"] + step) % count for step in (count - 1, 1)]
+    for side in sides:
+        pl.semaphore_signal(
+            barrier, inc=1, device_id=(place["mid"], side), device_id_type=pl.DeviceIdType.MESH
+        )
     for j in range(splits):
         cols = slice(j * wide, (j + 1) * wide)
         held[j * tall : (j + 1) * tall] = part_ref[:, cols].reshape(tall, 16, wide)
-    pl.semaphore_wait(barrier, steps)
+    pl.semaphore_wait(barrier, steps + 2)
+    edges = []
+    for e, side in enumerate(sides):
+        edges.append(
+            pltpu.make_async_remote_copy(
+                src_ref=edge_ref.at[pl.ds(e * BLOCK, BLOCK)],
+                dst_ref=edge_landed.at[pl.ds((1 - e) * BLOCK, BLOCK)],
+                send_sem=edge_send.at[e],
+                recv_sem=edge_recv.at[e],
+                device_id=(place["mid"], side),
+                device_id_type=pl.DeviceIdType.MESH,
+            )
+        )
 
     starts = [[None] * (steps + 1) for _ in orders]
     for c, order in enumerate(orders):
@@ -280,7 +313,7 @@
         return remote(mine, mine, c, steps + i, axis, bit)
 
     copies = [halve(c, 0) for c in range(chains)]
-    for copy in copies:
+    for copy in copies + edges:
         copy.start()
     for i in range(steps):
         size = span >> (i + 1)
@@ -305,25 +338,34 @@
     for j in range(splits):
         cols = slice(j * wide, (j + 1) * wide)
         out_ref[:, cols] = whole[j * tall : (j + 1) * tall].reshape(tall * 16, wide)
-
-
-def weight_sum(part, mid_size, off_size, scale):
+    for copy in edges:
+        copy.wait()
+    edge_out_ref[...] = edge_landed[...]
+
+
+def weight_sum(part, edges, mid_size, off_size, scale):
     rows, columns = part.shape
     orders = chain_orders(mid_size, off_size)
     steps = len(orders[0])
     splits = max(1, 16 * len(orders) * mid_size * off_size // rows)
     pieces, wide = splits * rows // 16, columns // splits
     return pl.pallas_call(
-        functools.partial(weight_sum_kernel, orders, scale),
-        out_shape=jax.ShapeDtypeStruct((rows, columns), jnp.bfloat16),
-        in_specs=[VMEM],
-        out_specs=VMEM,
+        functools.partial(weight_sum_kernel, orders, scale, off_size),
+        out_shape=(
+            jax.ShapeDtypeStruct((rows, columns), jnp.bfloat16),
+            jax.ShapeDtypeStruct(edges.shape, jnp.bfloat16),
+        ),
+        in_specs=[VMEM, VMEM],
+        out_specs=(VMEM, VMEM),
         scratch_shapes=[
             pltpu.VMEM((pieces, 16, wide), jnp.bfloat16),
             pltpu.VMEM((pieces, 16, wide), jnp.bfloat16),
             pltpu.VMEM((pieces, 16, wide), jnp.bfloat16),
+            pltpu.VMEM(edges.shape, jnp.bfloat16),
             pltpu.SemaphoreType.DMA((len(orders), 2 * steps)),
             pltpu.SemaphoreType.DMA((len(orders), 2 * steps)),
+            pltpu.SemaphoreType.DMA((2,)),
+            pltpu.SemaphoreType.DMA((2,)),
         ],
         compiler_params=pltpu.CompilerParams(
             vmem_limit_bytes=16 * 1024 * 1024, collective_id=0, has_side_effects=True
@@ -331,14 +373,7 @@
         cost_estimate=pl.CostEstimate(
             flops=2 * rows * columns, bytes_accessed=64 * rows * columns, transcendentals=0
         ),
-    )(part)
-
-
-def edge_swap(head, tail):
-    count = lax.axis_size("off")
-    before = lax.ppermute(tail, "off", [(i, i + 1) for i in range(count - 1)])
-    after = lax.ppermute(head, "off", [(i + 1, i) for i in range(count - 1)])
-    return before, after
+    )(part, edges)
 
 
 def on_device(query_rows, key_rows, value_rows, grad_out, out_weight, masked_rows, far_blocks):
@@ -428,9 +463,8 @@
         gathered.reshape(total_blocks, BLOCK, width),
     )
     inbound = exchange(outbound)
-    before, after = edge_swap(edges[:BLOCK], edges[BLOCK:])
     weight_scale = (row_count * mid_size * off_size) ** (-0.5)
-    weight_grad = weight_sum(weight_part, mid_size, off_size, weight_scale)
+    weight_grad, edge_in = weight_sum(weight_part, edges, mid_size, off_size, weight_scale)
     key_grad, value_grad = pl.pallas_call(
         functools.partial(finish_kernel, slot_total),
         out_shape=(jax.ShapeDtypeStruct((row_count, features), jnp.bfloat16),) * 2,
@@ -438,7 +472,7 @@
         out_specs=(VMEM,) * 2,
         scratch_shapes=[pltpu.VMEM((row_count, width), jnp.float32)],
         compiler_params=pltpu.CompilerParams(vmem_limit_bytes=VMEM_LIMIT),
-    )(chosen, filled, own, jnp.concatenate([before, after], axis=0), inbound)
+    )(chosen, filled, own, edge_in, inbound)
     return query_grad, key_grad, value_grad, weight_grad
 
 

time: 129 us -> 127 us (0.984)
  starting transfers between devices: 8.22 us -> 4.58 us
  Pallas kernels: 105 us -> 107 us
    ppermute x2 -> x0, starting transfers between devices: 3.65 us -> none  [the longest x1 2.36 us: edge_swap(): before = lax.ppermute(tail, 'off', [(i, i + 1) for i in range(count - 1)])]
    pallas_call x1, Pallas kernels: 47 us -> 48.6 us  [weight_sum(): pl.pallas_call(functools.partial(weight_sum_kernel, orders, scale, off_si...]
    unnamed x12 -> x18, local copies, waits for them, and re-layouts: 7.67 us -> 8.08 us
  transfers between devices with their start and end apart: 3 -> 1, of which waited for: 0 -> 0; matrix products, arithmetic and copies ran while one was open for 2% -> 1% of each run, Pallas kernels for 36% -> 38%
where the time goes in v5:
time: 127 us
  Pallas kernels  107 us (84%)
  local copies, waits for them, and re-layouts  11.7 us (9%)
  starting transfers between devices  4.58 us (4%)
  other arithmetic  2.96 us (2%)
    pallas_call x1, Pallas kernels, weight_sum(): pl.pallas_call(functools.partial(weight_sum_kernel, orders, scale, off_si...  48.6 us
    pallas_call x1, Pallas kernels, on_device(): pl.pallas_call(functools.partial(gather_kernel, off_size), out_shape=jax....  28.2 us
    pallas_call x1, Pallas kernels, on_device(): pl.pallas_call(functools.partial(attend_kernel, blocks, far_slots, slot_t...  25.9 us
    unnamed x18, local copies, waits for them, and re-layouts  8.08 us
    all_to_all x1, starting transfers between devices, exchange(): lax.all_to_all(parts, 'off', split_axis=0, concat_axis=0, tiled=True)  4.58 us
    pallas_call x1, Pallas kernels, on_device(): pl.pallas_call(functools.partial(finish_kernel, slot_total), out_shape=(j...  4.09 us
  transfers between devices with their start and end apart: 1, of which 0 were waited for; matrix products, arithmetic and copies ran while one was open for 1% of the time, Pallas kernels for 38%

profile of v5, /device:TPU:0, one launch (start us, length us, event | category | flops | bytes accessed | tf_op | source)
XLA Modules:
  0.0 126.8 jit_solution(14167319736312198957)
XLA Ops:
  0.7 0.5 fusion.14.near_ref
  1.2 0.7 convert_element_type.25
  1.8 0.8 copy.12
  2.6 0.1 reshape.117
  2.7 0.1 ne.121
  2.8 0.1 fusion
  2.9 0.2 select_reduce_fusion.1
  3.2 0.7 reshape.122.live_ref
  3.9 0.7 select_n.97.slot_ref
  4.5 0.1 rem.155
  4.6 0.1 div.63
  4.7 0.7 convert_element_type.31.mask_ref
  5.4 0.5 add_convert_fusion.edge_ref
  6.0 0.0 copy-start.4
  6.0 1.0 copy-done.4
  7.0 0.0 copy-start.5
  7.0 1.0 copy-done.5
  8.1 28.2 %shard_map.102 = bf16[8,4,32,2048]{3,2,1,0:T(8,128)(2,1)S(1)} custom-call(bf16[256,1024]{1,0:T(8,128)(2,1)S(1)} %copy-done.4, bf16[256,1024]{1,0:T(8,128)(2,1)S(1)} %copy-done.5), custom_call_target="tpu_custom_call" | custom-call | tf_op jit(solution)/shard_map/pallas_call | solution.py:415
  36.3 0.0 copy-start
  36.3 1.9 %copy-done = bf16[8,4,32,2048]{3,2,1,0:T(8,128)(2,1)} copy-done((bf16[8,4,32,2048]{3,2,1,0:T(8,128)(2,1)}, bf16[8,4,32,2048]{3,2,1,0:T(8,128)(2,1)S(1)}, u32[]{:S(2)}) %copy-start) | copy-done | bytes 4194328
  38.2 0.6 fusion.4.source_ref
  38.8 25.9 %shard_map.103 = (bf16[256,1024]{1,0:T(8,128)(2,1)}, f32[256,2048]{1,0:T(8,128)}, bf16[64,2048]{1,0:T(8,128)(2,1)}, bf16[16,32,2048]{2,1,0:T(8,128)(2,1)}, bf16[1024,1024]{1,0:T(8,128)(2,1)}) custom-call(s32[8,2]{1,0:T(8,128)} %select_n.97.slot_ref, s32[8,2]{1,0:T(8,128)} %reshape.122.live_ref, s32[2,8]{1,0:T(2,128)} %add_convert_fusion.edge_ref, ...), custom_call_target="tpu_custom_call" | custom-call | tf_op jit(solution)/shard_map/pallas_call | solution.py:434
  64.7 0.0 copy-start.1
  64.7 0.0 copy-start.6
  64.7 4.6 %all-to-all-start = ((bf16[4,4,32,2048]{3,2,1,0:T(8,128)(2,1)}), bf16[4,4,32,2048]{3,2,1,0:T(8,128)(2,1)}, u32[]{:S(2)}, u32[]{:S(2)}) async-start(bf16[4,4,32,2048]{3,2,1,0:T(8,128)(2,1)} %bitcast.4), calls=%async_computation | async-start | bytes 4194304 | tf_op jit(solution)/shard_map/all_to_all | solution.py:431
  69.3 0.1 select_reduce_fusion
  69.4 0.6 reshape.119.chosen_ref
  70.0 0.1 fusion.2
  70.1 0.6 reshape.123.filled_ref
  70.7 0.0 copy-done.1
  70.7 0.0 copy-done.6
  70.7 48.6 %shard_map.104 = (bf16[1024,1024]{1,0:T(8,128)(2,1)S(1)}, bf16[64,2048]{1,0:T(8,128)(2,1)S(1)}) custom-call(bf16[1024,1024]{1,0:T(8,128)(2,1)S(1)} %copy-done.1, bf16[64,2048]{1,0:T(8,128)(2,1)S(1)} %copy-done.6), custom_call_target="tpu_custom_call" | custom-call | flops 2097152 | bytes 67108864 | tf_op jit(solution)/shard_map/pallas_call | solution.py:352
  119.3 0.0 copy-start.2
  119.4 1.3 %copy-done.2 = bf16[1024,1024]{1,0:T(8,128)(2,1)} copy-done((bf16[1024,1024]{1,0:T(8,128)(2,1)}, bf16[1024,1024]{1,0:T(8,128)(2,1)S(1)}, u32[]{:S(2)}) %copy-start.2) | copy-done | bytes 2097176
  120.6 0.0 copy-start.7
  120.6 0.7 copy-done.7
  121.3 0.0 all-to-all-done
  121.4 0.0 copy-start.3
  121.4 4.1 %shard_map.105 = (bf16[256,1024]{1,0:T(8,128)(2,1)}, bf16[256,1024]{1,0:T(8,128)(2,1)}) custom-call(s32[16]{0:T(128)} %reshape.119.chosen_ref, s32[16]{0:T(128)} %reshape.123.filled_ref, f32[256,2048]{1,0:T(8,128)} %get-tuple-element.14.own_ref, bf16[64,2048]{1,0:T(8,128)(2,1)} %copy-done.7, bf16[16,32,2048]{2,1,0:T(8,128)(2,1)} %bitcast.2.inbound_ref), custom_call_target="tpu_custom_call" | custom-call | tf_op jit(solution)/shard_map/pallas_call | solution.py:468
  125.4 0.0 copy-done.3
  125.5 1.3 %copy.15 = bf16[1024,1024]{1,0:T(8,128)(2,1)} copy(bf16[1024,1024]{1,0:T(8,128)(2,1)S(1)} %copy-done.3) | data formatting | bytes 4194304
  (7 shorter events, 0.1 us)
Async XLA Ops:
  6.0 1.0 copy-start.4
  7.0 1.0 copy-start.5
  36.3 1.9 %copy-start = (bf16[8,4,32,2048]{3,2,1,0:T(8,128)(2,1)}, bf16[8,4,32,2048]{3,2,1,0:T(8,128)(2,1)S(1)}, u32[]{:S(2)}) copy-start(bf16[8,4,32,2048]{3,2,1,0:T(8,128)(2,1)S(1)} %shard_map.102) | copy-start | bytes 12582916
  64.7 6.0 %copy-start.1 = (bf16[1024,1024]{1,0:T(8,128)(2,1)S(1)}, bf16[1024,1024]{1,0:T(8,128)(2,1)}, u32[]{:S(2)}) copy-start(bf16[1024,1024]{1,0:T(8,128)(2,1)} %get-tuple-element.15.part_ref) | copy-start | bytes 6291460
  64.7 6.0 %copy-start.6 = (bf16[64,2048]{1,0:T(8,128)(2,1)S(1)}, bf16[64,2048]{1,0:T(8,128)(2,1)}, u32[]{:S(2)}) copy-start(bf16[64,2048]{1,0:T(8,128)(2,1)} %get-tuple-element.16.edge_ref) | copy-start | bytes 786436
  64.7 56.6 %all-to-all-start = ((bf16[4,4,32,2048]{3,2,1,0:T(8,128)(2,1)}), bf16[4,4,32,2048]{3,2,1,0:T(8,128)(2,1)}, u32[]{:S(2)}, u32[]{:S(2)}) async-start(bf16[4,4,32,2048]{3,2,1,0:T(8,128)(2,1)} %bitcast.4), calls=%async_computation | async-start | bytes 4194304 | tf_op jit(solution)/shard_map/all_to_all | solution.py:431
  119.3 1.3 %copy-start.2 = (bf16[1024,1024]{1,0:T(8,128)(2,1)}, bf16[1024,1024]{1,0:T(8,128)(2,1)S(1)}, u32[]{:S(2)}) copy-start(bf16[1024,1024]{1,0:T(8,128)(2,1)S(1)} %get-tuple-element.40) | copy-start | bytes 6291460
  120.6 0.7 copy-start.7
  121.4 4.1 %copy-start.3 = (bf16[1024,1024]{1,0:T(8,128)(2,1)S(1)}, bf16[1024,1024]{1,0:T(8,128)(2,1)}, u32[]{:S(2)}) copy-start(bf16[1024,1024]{1,0:T(8,128)(2,1)} %copy-done.2) | copy-start | bytes 6291460
